TPU v7x, 256 devices: a whole 4x4x8 slice. The times are simulated.
256 devices in a mesh: grid: 64 (over y, x_hi, z), heads: 4 (over x_lo, core).
Axes of the slice: x: 4 (x_hi: 2, x_lo: 2; x = x_hi * 2 + x_lo), y: 4, z: 8, core: 2. Of those that a mesh axis runs over, the one named last changes fastest.
Arguments:
- tokens: bfloat16 [64, 8, 64, 1024], P('grid', None, None, 'heads'), may hold values from -16 to 16
- qkv_weight: bfloat16 [3, 1024, 1024], P(None, None, 'heads'), may hold values from -0.1875 to 0.1875
- out_weight: bfloat16 [1024, 1024], P('heads'), may hold values from -0.1875 to 0.1875
- out_grad: bfloat16 [64, 8, 64, 1024], P('grid', None, None, 'heads'), may hold values from -16 to 16
Outputs:
- d_tokens: bfloat16 [64, 8, 64, 1024], P('grid', None, None, 'heads')
- d_qkv_weight: float32 [3, 1024, 1024], P(None, 'grid', 'heads')
- d_out_weight: float32 [1024, 1024], P('heads', 'grid')
All inputs are finite; a program needn't handle non-finite values.
Results may differ from a plain program's by a relative error of at most 0.023.
Values may be sent and summed in bfloat16 or wider, within the bound.
A program may use at most 128 MiB of HBM per device.

v0:
```python
import jax
import jax.numpy as jnp
from jax import lax
from jax.sharding import PartitionSpec as P

HD = 64
RADIUS = 6
LON_TILES = 8


band_rows = 8


def from_behind(value, axis, steps):
    count = lax.axis_size(axis)
    pairs = [(source, (source + steps) % count) for source in range(count)]
    return lax.ppermute(value, axis, pairs)


def neighbour(values_in, shift_by):
    return from_behind(values_in, "grid", shift_by)


def returned(values_in, shift_by):
    return from_behind(values_in, "grid", shift_by)


def inner_slice(length, side_step):
    if side_step == -1:
        return slice(length - RADIUS, length)
    return slice(0, RADIUS)


def outer_slice(length, side_step):
    if side_step == -1:
        return slice(0, RADIUS)
    return slice(RADIUS + length, length + 2 * RADIUS)


def masked(values_in, keep_flag):
    return jnp.where(keep_flag, values_in, jnp.zeros_like(values_in))


def extend_rims(keyval, lat_count, has_north, bottom):
    tile_rows, tile_cols, feature_count = keyval.shape
    west_rim = neighbour(keyval[:, inner_slice(tile_cols, -1)], lat_count)
    east_rim = neighbour(keyval[:, inner_slice(tile_cols, 1)], -lat_count)
    widened = jnp.concatenate([west_rim, keyval, east_rim], axis=1)
    north_rim = masked(neighbour(widened[inner_slice(tile_rows, -1)], 1), has_north)
    south_rim = masked(neighbour(widened[inner_slice(tile_rows, 1)], -1), bottom)
    return jnp.concatenate([north_rim, widened, south_rim], axis=0)


def fold_back(grads_ext, lat_count, has_north, bottom):
    tile_rows = grads_ext.shape[0] - 2 * RADIUS
    tile_cols = grads_ext.shape[1] - 2 * RADIUS
    widened = grads_ext[RADIUS : RADIUS + tile_rows]
    from_south = masked(returned(grads_ext[outer_slice(tile_rows, -1)], -1), bottom)
    widened = widened.at[inner_slice(tile_rows, -1)].add(from_south)
    from_north = masked(returned(grads_ext[outer_slice(tile_rows, 1)], 1), has_north)
    widened = widened.at[inner_slice(tile_rows, 1)].add(from_north)
    interior = widened[:, RADIUS : RADIUS + tile_cols]
    from_east = returned(widened[:, outer_slice(tile_cols, -1)], -lat_count)
    interior = interior.at[:, inner_slice(tile_cols, -1)].add(from_east)
    from_west = returned(widened[:, outer_slice(tile_cols, 1)], lat_count)
    interior = interior.at[:, inner_slice(tile_cols, 1)].add(from_west)
    return interior


def local(tokens, qkv_weight, out_weight, out_grad):
    tile_rows, tile_cols, local_width = (tokens.shape[1], tokens.shape[2], tokens.shape[3])
    patch_count = tile_rows * tile_cols
    heads_here = local_width // HD
    score_scale = HD ** (-0.5)
    full_tokens, full_grad = (
        lax.all_gather(tokens, "heads", axis=3, tiled=True),
        lax.all_gather(out_grad, "heads", axis=3, tiled=True),
    )
    model_width = full_tokens.shape[3]
    token_rows = full_tokens.reshape(patch_count, model_width)
    grad_rows = full_grad.reshape(patch_count, model_width)
    projected = jnp.einsum(
        "nd,cde->cne", token_rows, qkv_weight, preferred_element_type=jnp.float32
    ).astype(jnp.bfloat16)
    queries = projected[0].reshape(tile_rows, tile_cols, local_width)
    keyval = jnp.concatenate([projected[1], projected[2]], axis=1).reshape(
        tile_rows, tile_cols, 2 * local_width
    )
    d_out = lax.dot_general(
        grad_rows, out_weight, (((1,), (1,)), ((), ())), preferred_element_type=jnp.float32
    )
    d_out = d_out.astype(jnp.bfloat16).reshape(tile_rows, tile_cols, local_width)
    lat_count = lax.axis_size("grid") // LON_TILES
    lat_here = lax.axis_index("grid") % lat_count
    has_north = lat_here > 0
    bottom = lat_here < lat_count - 1
    extended = extend_rims(keyval, lat_count, has_north, bottom)
    positions = jnp.arange(tile_rows + 2 * RADIUS)
    row_valid = ((positions >= RADIUS) | has_north) & ((positions < RADIUS + tile_rows) | bottom)
    window = band_rows + 2 * RADIUS
    block_count = tile_cols // band_rows
    query_pos = jnp.arange(band_rows)
    key_pos = jnp.arange(window)
    reach = key_pos[None, :] - query_pos[:, None]
    inside = (reach >= 0) & (reach <= 2 * RADIUS)

    def to_blocks(values_in):
        split_up = values_in.reshape(band_rows, block_count, band_rows, heads_here, HD)
        return split_up.transpose(1, 0, 2, 3, 4).reshape(
            block_count, band_rows * band_rows, heads_here, HD
        )

    def from_blocks(values_in):
        split_up = values_in.reshape(block_count, band_rows, band_rows, local_width)
        return split_up.transpose(1, 0, 2, 3).reshape(band_rows, tile_cols, local_width)

    def band_step(band_index, carried):
        grads_ext, attended_all, d_query_all = carried
        windows = jnp.stack(
            [
                extended[:, block_col * band_rows : block_col * band_rows + window]
                for block_col in range(block_count)
            ]
        )
        windows = windows.reshape(block_count, window * window, 2 * local_width)
        key_block = windows[..., :local_width].reshape(block_count, window * window, heads_here, HD)
        value_block = windows[..., local_width:].reshape(
            block_count, window * window, heads_here, HD
        )
        query_block = to_blocks(queries)
        grad_block = to_blocks(d_out)
        allowed = (
            inside[:, None, :, None] & inside[None, :, None, :] & row_valid[None, None, :, None]
        )
        allowed = allowed.reshape(band_rows * band_rows, window * window)
        scores = (
            jnp.einsum(
                "wqhe,wkhe->whqk", query_block, key_block, preferred_element_type=jnp.float32
            )
            * score_scale
        )
        weights_raw = jnp.where(allowed, jnp.exp(scores), 0.0)
        softmax = weights_raw / jnp.sum(weights_raw, axis=-1, keepdims=True)
        softmax_b = softmax.astype(jnp.bfloat16)
        attended = jnp.einsum(
            "whqk,wkhe->wqhe", softmax_b, value_block, preferred_element_type=jnp.float32
        ).astype(jnp.bfloat16)
        d_probs = jnp.einsum(
            "wqhe,wkhe->whqk", grad_block, value_block, preferred_element_type=jnp.float32
        )
        row_delta = jnp.einsum(
            "wqhe,wqhe->whq", grad_block, attended, preferred_element_type=jnp.float32
        )
        d_scores = (softmax * (d_probs - row_delta[..., None])).astype(jnp.bfloat16)
        d_query = (
            jnp.einsum("whqk,wkhe->wqhe", d_scores, key_block, preferred_element_type=jnp.float32)
            * score_scale
        )
        d_key = (
            jnp.einsum("whqk,wqhe->wkhe", d_scores, query_block, preferred_element_type=jnp.float32)
            * score_scale
        )
        d_value = jnp.einsum(
            "whqk,wqhe->wkhe", softmax_b, grad_block, preferred_element_type=jnp.float32
        )
        key_value_grads = jnp.concatenate(
            [
                d_key.reshape(block_count, window, window, local_width),
                d_value.reshape(block_count, window, window, local_width),
            ],
            axis=-1,
        )
        band_grads = jnp.zeros((window, tile_cols + 2 * RADIUS, 2 * local_width), jnp.float32)
        for block_col in range(block_count):
            band_grads = band_grads.at[
                :, block_col * band_rows : block_col * band_rows + window
            ].add(key_value_grads[block_col])
        current = grads_ext
        grads_ext = current + band_grads
        attended_all = from_blocks(attended)
        d_query_all = from_blocks(d_query)
        return (grads_ext, attended_all, d_query_all)

    start_state = (
        jnp.zeros((tile_rows + 2 * RADIUS, tile_cols + 2 * RADIUS, 2 * local_width), jnp.float32),
        jnp.zeros((tile_rows, tile_cols, local_width), jnp.bfloat16),
        jnp.zeros((tile_rows, tile_cols, local_width), jnp.float32),
    )
    grads_ext, attended_all, d_query_all = lax.fori_loop(
        0, tile_rows // band_rows, band_step, start_state
    )
    interior = fold_back(grads_ext, lat_count, has_north, bottom)
    d_proj = jnp.stack(
        [
            d_query_all.reshape(patch_count, local_width),
            interior[..., :local_width].reshape(patch_count, local_width),
            interior[..., local_width:].reshape(patch_count, local_width),
        ]
    ).astype(jnp.bfloat16)
    attended_rows = attended_all.reshape(patch_count, local_width)
    qkv_term = jnp.einsum("nd,cne->cde", token_rows, d_proj, preferred_element_type=jnp.float32)
    out_term = lax.dot_general(
        attended_rows, grad_rows, (((0,), (0,)), ((), ())), preferred_element_type=jnp.float32
    )
    d_qkv_weight, d_out_weight = (
        lax.psum_scatter(qkv_term, "grid", scatter_dimension=1, tiled=True),
        lax.psum_scatter(out_term, "grid", scatter_dimension=1, tiled=True),
    )
    partial_sum = jnp.einsum("cne,cde->nd", d_proj, qkv_weight, preferred_element_type=jnp.float32)
    d_rows = lax.psum_scatter(partial_sum, "heads", scatter_dimension=1, tiled=True).astype(
        jnp.bfloat16
    )
    return (d_rows.reshape(1, tile_rows, tile_cols, local_width), d_qkv_weight, d_out_weight)


def solution(mesh):
    in_specs = (
        P("grid", None, None, "heads"),
        P(None, None, "heads"),
        P("heads", None),
        P("grid", None, None, "heads"),
    )
    out_specs = (P("grid", None, None, "heads"), P(None, "grid", "heads"), P("heads", "grid"))
    return jax.shard_map(local, mesh=mesh, in_specs=in_specs, out_specs=out_specs, check_vma=False)
```

profile of v0, /device:TPU:2, one launch (start us, length us, event | category | flops | bytes accessed | tf_op | source)
XLA Modules:
  0.0 1384.3 jit_solution(3403523221158869711)
XLA Ops:
  9.4 26.7 %all-gather.3.cloned.1.call-done = bf16[1,8,64,1024]{3,2,1,0:T(8,128)(2,1)} async-done(((bf16[1,8,64,256]{3,2,1,0:T(8,128)(2,1)}), bf16[1,8,64,1024]{3,2,1,0:T(8,128)(2,1)}) %all-gather.3.cloned.1.call-update) | async-done | bytes 1048592 | tf_op jit(solution)/shard_map/all_gather | solution.py:76
  49.9 23.4 %all-gather.5.cloned.1.call-done = bf16[1,8,64,1024]{3,2,1,0:T(8,128)(2,1)} async-done(((bf16[1,8,64,256]{3,2,1,0:T(8,128)(2,1)}), bf16[1,8,64,1024]{3,2,1,0:T(8,128)(2,1)}) %all-gather.5.cloned.1.call-update) | async-done | bytes 1048592 | tf_op jit(solution)/shard_map/all_gather | solution.py:77
  79.9 11.3 collective-permute-done.3
  110.7 3.7 copy.40
  130.8 7.9 copy.69
  138.7 8.1 reshape.602
  146.8 7.9 copy.70
  154.7 8.1 reshape.603
  172.1 5.8 scatter-add.49
  179.7 5.8 scatter-add.52
  187.2 5.8 scatter-add.53
  194.7 5.8 scatter-add.54
  202.2 5.8 scatter-add.57
  209.7 5.7 scatter-add.58
  219.9 5.1 collective-permute-start.4
  225.1 20.8 %collective-permute-done.4 = f32[6,76,512]{2,1,0:T(8,128)S(1)} collective-permute-done((f32[6,76,512]{2,1,0:T(8,128)S(1)}, f32[6,76,512]{2,1,0:T(8,128)S(1)}, u32[]{:S(2)}, u32[]{:S(2)}) %collective-permute-start.4) | collective-permute-done | bytes 933920 | tf_op jit(solution)/shard_map/ppermute | solution.py:17
  246.1 7.7 collective-permute-done.5
  259.3 3.5 collective-permute-start.7
  264.5 3.7 collective-permute-done.7
  272.1 3.9 convolution_bitcast_fusion.1
  276.0 5.0 copy.54
  288.1 691.2 %all-reduce.4.cloned.1.call-done = f32[3,1024,256]{2,0,1:T(4,128)} async-done(((f32[3,1024,256]{2,0,1:T(4,128)}), f32[3,1024,256]{2,0,1:T(4,128)}) %all-reduce.4.cloned.1.call-update) | async-done | bytes 3145744
  980.8 28.3 %reduce-scatter.3.cloned.1.call-done = f32[512,256]{1,0:T(8,128)} async-done(((f32[512,1024]{1,0:T(8,128)}), f32[512,256]{1,0:T(8,128)}) %reduce-scatter.3.cloned.1.call-update) | async-done | bytes 524304 | tf_op jit(solution)/shard_map/reduce_scatter | solution.py:210
  1010.8 367.0 %reduce-scatter.5.cloned.1.call-done = f32[256,16]{0,1:T(8,128)} async-done(((f32[256,1024]{0,1:T(8,128)}), f32[256,16]{0,1:T(8,128)}) %reduce-scatter.5.cloned.1.call-update) | async-done | bytes 16400 | tf_op jit(solution)/shard_map/reduce_scatter | solution.py:207
  (139 shorter events, 101.5 us)
Async XLA Ops:
  7.2 29.0 %copy-start = (bf16[3,1024,256]{2,1,0:T(8,128)(2,1)S(1)}, bf16[3,1024,256]{2,1,0:T(8,128)(2,1)}, u32[]{:S(2)}) copy-start(bf16[3,1024,256]{2,1,0:T(8,128)(2,1)} %param.29) | copy-start | bytes 4718596
  7.2 29.0 %all-gather.3.cloned.1.call-start = ((), (), s32[]{:S(2)}) async-start(), calls=%async_computation.2 | async-start | bytes 1310720 | tf_op jit(solution)/shard_map/all_gather | solution.py:76
  7.9 65.3 %all-gather.5.cloned.1.call-start = ((), (), s32[]{:S(2)}) async-start(), calls=%async_computation.3 | async-start | bytes 1310720 | tf_op jit(solution)/shard_map/all_gather | solution.py:77
  8.7 970.6 %all-reduce.4.cloned.1.call-start = ((), (), s32[]{:S(2)}) async-start(), calls=%async_computation.6 | async-start | bytes 8388608
  38.8 8.1 collective-permute-start
  41.0 6.1 collective-permute-start.1
  48.3 31.5 %collective-permute-start.2 = (bf16[6,76,512]{2,1,0:T(8,128)(2,1)}, bf16[6,76,512]{2,1,0:T(8,128)(2,1)}, u32[]{:S(2)}, u32[]{:S(2)}) collective-permute-start(bf16[6,76,512]{2,1,0:T(8,128)(2,1)} %get-tuple-element.238), channel_id=1, source_target_pairs={{0,4},{4,8},{8,12},{12,16},{16,20},{20,24},{24,28},{28,32},{32,36}... | collective-permute-start | bytes 1400840 | tf_op jit(solution)/shard_map/ppermute | solution.py:17
  77.3 13.8 collective-permute-start.3
  102.3 6.8 copy-start.12
  103.2 6.0 copy-start.11
  104.0 5.2 copy-start.10
  104.9 4.2 copy-start.13
  110.7 6.3 copy-start.16
  162.9 3.3 copy-start.3
  218.0 6.9 copy-start.1
  219.9 26.1 %collective-permute-start.4 = (f32[6,76,512]{2,1,0:T(8,128)S(1)}, f32[6,76,512]{2,1,0:T(8,128)S(1)}, u32[]{:S(2)}, u32[]{:S(2)}) collective-permute-start(f32[6,76,512]{2,1,0:T(8,128)S(1)} %get-tuple-element.222), channel_id=1, source_target_pairs={{0,252},{4,0},{8,4},{12,8},{16,12},{20,16},{24,20},{28,24},{32,28}... | collective-permute-start | bytes 2801672 | tf_op jit(solution)/shard_map/ppermute | solution.py:17
  224.9 28.9 %collective-permute-start.5 = (f32[6,76,512]{2,1,0:T(8,128)S(1)}, f32[6,76,512]{2,1,0:T(8,128)S(1)}, u32[]{:S(2)}, u32[]{:S(2)}) collective-permute-start(f32[6,76,512]{2,1,0:T(8,128)S(1)} %get-tuple-element.221), channel_id=1, source_target_pairs={{0,4},{4,8},{8,12},{12,16},{16,20},{20,24},{24,28},{28,32},{32,36}... | collective-permute-start | bytes 2801672 | tf_op jit(solution)/shard_map/ppermute | solution.py:17
  225.1 29.8 %copy-start.4 = (bf16[8,400,256]{1,2,0:T(8,128)(2,1)S(1)}, bf16[8,400,256]{1,2,0:T(8,128)(2,1)}, u32[]{:S(2)}) copy-start(bf16[8,400,256]{1,2,0:T(8,128)(2,1)} %copy.40) | copy-start | bytes 4915204
  225.1 29.8 %copy-start.6 = (bf16[8,4,64,400]{3,2,1,0:T(8,128)(2,1)S(1)}, bf16[8,4,64,400]{3,2,1,0:T(8,128)(2,1)}, u32[]{:S(2)}) copy-start(bf16[8,4,64,400]{3,2,1,0:T(8,128)(2,1)} %copy-done.5) | copy-start | bytes 4915204
  254.9 8.0 collective-permute-start.6
  259.3 8.8 collective-permute-start.7
  281.0 728.1 %reduce-scatter.3.cloned.1.call-start = ((), (), s32[]{:S(2)}) async-start(), calls=%async_computation.4 | async-start | bytes 2621440 | tf_op jit(solution)/shard_map/reduce_scatter | solution.py:210
  283.5 3.4 copy-start.17
  283.5 1094.3 %reduce-scatter.5.cloned.1.call-start = ((), (), s32[]{:S(2)}) async-start(), calls=%async_computation.5 | async-start | bytes 1064960 | tf_op jit(solution)/shard_map/reduce_scatter | solution.py:207
  (7 other events, 17.9 us)
Sparse Core Ops, SparseCore 0:
  9.8 26.2 all-gather.2
  37.9 35.2 all-gather.4
  281.1 698.1 all-reduce.3
  981.9 27.1 reduce-scatter.2
  1012.0 365.8 reduce-scatter.4
where the time goes:
time: 1390 us; the launch traced here: 1380 us
  waiting for transfers between devices  1180 us (85%)
  local copies, waits for them, and re-layouts  126 us (9%)
  matrix products  25 us (2%)
  other arithmetic  19.3 us (1%)
  starting transfers between devices  16.1 us (1%)
  between operations  14.9 us (1%)
    unnamed x6, waiting for transfers between devices  693 us
    reduce_scatter x1, waiting for transfers between devices, local(): lax.psum_scatter(out_term, 'grid', scatter_dimension=1, tiled=True)  367 us
    ppermute x8, waiting for transfers between devices, from_behind(): return lax.ppermute(value, axis, pairs)  45.5 us
    scatter-add x7, local copies, waits for them, and re-layouts, band_step(): band_grads = band_grads.at[:, block_col * band_rows:block_col * band_rows...  36.9 us
    reduce_scatter x1, waiting for transfers between devices, local(): lax.psum_scatter(partial_sum, 'heads', scatter_dimension=1, tiled=True)  28.3 us
  transfers between devices with their start and end apart: 13, of which 11 were waited for; matrix products, arithmetic and copies ran while one was open for 2% of the time, Pallas kernels for 0%

commit v1 on v0

v1 whole, which is shorter than its diff:
```python
import jax
import jax.numpy as jnp
from jax import lax
from jax.experimental import pallas as pl
from jax.experimental.pallas import tpu as pltpu
from jax.sharding import PartitionSpec as P

MESH = pl.DeviceIdType.MESH
F32 = jnp.float32
BF16 = jnp.bfloat16

HD = 64
RAD = 6
LON = 8
LAT = 8
TH = 8
TW = 64
WID = 256
ROWS = TH * TW
EXT_R = TH + 2 * RAD
PAD = 8
EXT_C = TW + 2 * PAD
BW = 16
WINC = BW + 2 * PAD
KEYS = EXT_R * WINC
QN = TH * BW
SLAB = RAD * TW
EDGE = TH * PAD
CORNER = RAD * PAD

WAYS = ((-1, 0), (1, 0), (0, -1), (0, 1), (-1, -1), (-1, 1), (1, -1), (1, 1))


def mm(a, b, ca=1, cb=0):
    return lax.dot_general(a, b, (((ca,), (cb,)), ((), ())), preferred_element_type=F32)


def kernel(
    x_ref, g_ref, w_any, wo_any,
    tok_ref, eo_ref, lo_ref,
    w_v, wo_v, xf, gf, acc, kvb, edge, ns_r, ew_r, dg_r, kvx, gx,
    q_s, do_s, o_s, dq_s, dkv, bias, xt, gt,
    gns_s, gew_s, gdg_s, gns_r, gew_r, gdg_r,
    e_s, e_r, l_s, l_r, own_e, own_l, pe_b, pl_b, e2_r, l2_r,
    tacc, t_s, t_r,
    w_sem, ag_ss, ag_rs, h_ss, h_rs, b_ss, b_rs,
    e_ss, e_rs, l_ss, l_rs, e2_ss, e2_rs, l2_ss, l2_rs, t_ss, t_rs,
):
    g = lax.axis_index("grid")
    h = lax.axis_index("heads")
    lat = lax.rem(g, LAT)
    lon = lax.div(g, LAT)
    sib = h + 1 - 2 * lax.rem(h, 2)
    far = h + 2 - 4 * lax.div(h, 2)
    opp = 3 - h
    slots = (h, sib, far, opp)

    w_copy = pltpu.make_async_copy(w_any, w_v, w_sem.at[0])
    wo_copy = pltpu.make_async_copy(wo_any, wo_v, w_sem.at[1])
    w_copy.start()
    wo_copy.start()

    def tile(dlat, dlon):
        return lax.rem(lon + dlon + LON, LON) * LAT + lax.rem(lat + dlat + LAT, LAT)

    def can_send(way):
        dlat = WAYS[way][0]
        return (lat + dlat >= 0) & (lat + dlat < LAT)

    def can_recv(way):
        dlat = WAYS[way][0]
        return (lat - dlat >= 0) & (lat - dlat < LAT)

    def when(cond_way, way, fn):
        if WAYS[way][0] == 0:
            fn()
        else:
            pl.when(cond_way(way))(fn)

    bar = pltpu.get_barrier_semaphore()

    def greet(to_grid, to_head):
        pl.semaphore_signal(bar, inc=1, device_id=(to_grid, to_head), device_id_type=MESH)

    greet(g, sib)
    greet(g, far)
    for k in range(1, 8):
        greet(tile(k, 0), h)
        greet(tile(0, k), h)
    for way in range(4, 8):
        when(can_send, way, lambda way=way: greet(tile(*WAYS[way]), h))
    has_n = (lat > 0).astype(jnp.int32)
    has_s = (lat < LAT - 1).astype(jnp.int32)
    pl.semaphore_wait(bar, 16 + 2 * has_n + 2 * has_s)

    def rcopy(src, dst, ss, rs, to_grid, to_head):
        return pltpu.make_async_remote_copy(
            src_ref=src, dst_ref=dst, send_sem=ss, recv_sem=rs,
            device_id=(to_grid, to_head), device_id_type=MESH,
        )

    def gather(src, full, base):
        return (
            rcopy(src, full.at[0], ag_ss.at[base], ag_rs.at[base], g, sib),
            rcopy(src, full.at[1], ag_ss.at[base + 1], ag_rs.at[base + 1], g, far),
            rcopy(full.at[1], full.at[2], ag_ss.at[base + 2], ag_rs.at[base + 2], g, sib),
        )

    x_sib, x_far, x_fwd = gather(x_ref, xf, 0)
    g_sib, g_far, g_fwd = gather(g_ref, gf, 3)
    x_far.start()
    x_sib.start()
    w_copy.wait()

    def add_kv(block, k):
        for c in range(2):
            part = mm(block, w_v[c + 1, slots[k]])
            cols = slice(c * WID, (c + 1) * WID)
            acc[:, cols] = part if k == 0 else acc[:, cols] + part

    add_kv(x_ref[...], 0)
    x_sib.wait_recv()
    add_kv(xf[0], 1)
    x_far.wait_recv()
    x_fwd.start()
    g_far.start()
    g_sib.start()
    add_kv(xf[1], 2)
    x_fwd.wait_recv()
    add_kv(xf[2], 3)

    def round_kv(i, carry):
        rows = pl.ds(pl.multiple_of(i * TW, TW), TW)
        value = acc[rows, :].astype(BF16)
        kvb[rows, :] = value
        kvx[i + RAD, PAD : PAD + TW, :] = value.astype(F32)
        return carry

    lax.fori_loop(0, TH, round_kv, 0)

    def halo_copy(way, srcs, dsts, ss, rs):
        dlat, dlon = WAYS[way]
        return rcopy(srcs[way], dsts[way], ss.at[way], rs.at[way], tile(dlat, dlon), h)

    halo_dst = [ns_r.at[0], ns_r.at[1], ew_r.at[0], ew_r.at[1]] + [dg_r.at[i] for i in range(4)]
    halo_src = [
        kvb.at[0:SLAB],
        kvb.at[ROWS - SLAB : ROWS],
        edge.at[0],
        edge.at[1],
        edge.at[0, 0:CORNER],
        edge.at[1, 0:CORNER],
        edge.at[0, EDGE - CORNER : EDGE],
        edge.at[1, EDGE - CORNER : EDGE],
    ]
    halo = [halo_copy(way, halo_src, halo_dst, h_ss, h_rs) for way in range(8)]
    for way in range(2):
        when(can_send, way, halo[way].start)
    body = slice(RAD, RAD + TH)
    edge[0] = kvx[body, PAD : 2 * PAD, :].reshape(EDGE, 2 * WID).astype(BF16)
    edge[1] = kvx[body, TW : TW + PAD, :].reshape(EDGE, 2 * WID).astype(BF16)
    for way in range(2, 8):
        when(can_send, way, halo[way].start)

    x_blocks = (x_ref, xf.at[0], xf.at[1], xf.at[2])
    g_blocks = (g_ref, gf.at[0], gf.at[1], gf.at[2])
    left = acc.at[:, 0:WID]
    for k in range(4):
        part = mm(x_blocks[k][...], w_v[0, slots[k]])
        left[...] = part if k == 0 else left[...] + part
    q_s[...] = (left[...].astype(BF16) * jnp.asarray(HD**-0.5, BF16)).reshape(TH, TW, WID)

    def turn(blocks, out):
        for k in range(4):
            for j in range(2):
                piece = blocks[k][:, j * 128 : (j + 1) * 128].astype(F32)
                out[2 * slots[k] + j] = piece.T.astype(BF16)

    g_sib.wait_recv()
    g_far.wait_recv()
    g_fwd.start()
    turn(x_blocks, xt)

    key = lax.broadcasted_iota(jnp.int32, (KEYS, QN), 0)
    qry = lax.broadcasted_iota(jnp.int32, (KEYS, QN), 1)
    key_r, key_c = lax.div(key, WINC), lax.rem(key, WINC)
    dr = key_r - lax.div(qry, BW)
    dc = key_c - lax.rem(qry, BW)
    at_lat = key_r + (lat * TH - RAD)
    fine = (dr >= 0) & (dr <= 2 * RAD) & (dc >= PAD - RAD) & (dc <= PAD + RAD)
    fine = fine & (at_lat >= 0) & (at_lat < LAT * TH)
    bias[...] = jnp.where(fine, 0.0, -1e30)

    def clear(i, carry):
        gx[i] = jnp.zeros((EXT_C, 2 * WID), F32)
        return carry

    lax.fori_loop(0, EXT_R, clear, 0)

    wo_copy.wait()
    g_fwd.wait_recv()
    for k in range(4):
        cols = pl.ds(pl.multiple_of(slots[k] * WID, WID), WID)
        part = mm(g_blocks[k][...], wo_v[:, cols], 1, 1)
        left[...] = part if k == 0 else left[...] + part
    do_s[...] = left[...].astype(BF16).reshape(TH, TW, WID)
    turn(g_blocks, gt)

    def ext_at(way):
        dlat, dlon = WAYS[way]
        rows = {-1: slice(RAD + TH, EXT_R), 1: slice(0, RAD), 0: body}[dlat]
        cols = {-1: slice(PAD + TW, EXT_C), 1: slice(0, PAD), 0: slice(PAD, PAD + TW)}[dlon]
        return rows, cols

    def shape_of(rows, cols):
        return rows.stop - rows.start, cols.stop - cols.start, 2 * WID

    for way in range(8):
        rows, cols = ext_at(way)
        shape = shape_of(rows, cols)

        def take(way=way, rows=rows, cols=cols, shape=shape):
            halo[way].wait_recv()
            kvx[rows, cols, :] = halo_dst[way][...].astype(F32).reshape(shape)

        def blank(rows=rows, cols=cols, shape=shape):
            kvx[rows, cols, :] = jnp.zeros(shape, F32)

        when(can_recv, way, take)
        if WAYS[way][0] != 0:
            pl.when(jnp.logical_not(can_recv(way)))(blank)

    lane = lax.broadcasted_iota(jnp.int32, (QN, 128), 1)
    first = lane < HD

    def two_heads(value):
        zero = jnp.zeros_like(value)
        return jnp.concatenate([jnp.where(first, value, zero), jnp.where(first, zero, value)], axis=0)

    def untwo(value):
        picked = jnp.concatenate([value[:HD, :QN], value[HD:, QN:]], axis=0)
        return picked.T.astype(BF16).reshape(TH, BW, 128)

    def block(b, carry):
        start = pl.multiple_of(b * BW, BW)
        mine = pl.ds(start, BW)
        window = pl.ds(start, WINC)
        for p in range(2):
            cols = slice(p * 128, (p + 1) * 128)
            vcols = slice(WID + p * 128, WID + (p + 1) * 128)
            keys = kvx[:, window, cols].reshape(KEYS, 128).astype(BF16)
            vals = kvx[:, window, vcols].reshape(KEYS, 128).astype(BF16)
            qq = two_heads(q_s[:, mine, cols].reshape(QN, 128))
            dd = two_heads(do_s[:, mine, cols].reshape(QN, 128))
            scores = mm(keys, qq, 1, 1)
            b1 = bias[...]
            raw = jnp.exp(scores + jnp.concatenate([b1, b1], axis=1))
            prob = raw * (1.0 / jnp.sum(raw, axis=0, keepdims=True))
            prob_b = prob.astype(BF16)
            d_prob = mm(vals, dd, 1, 1)
            delta = jnp.sum(prob * d_prob, axis=0, keepdims=True)
            d_sc = (prob * (d_prob - delta)).astype(BF16)
            o_s[:, mine, cols] = untwo(mm(vals, prob_b, 0, 0))
            dq_s[:, mine, cols] = untwo(mm(keys, d_sc, 0, 0) * HD**-0.5)
            gx[:, window, cols] += mm(d_sc, qq).reshape(EXT_R, WINC, 128)
            gx[:, window, vcols] += mm(prob_b, dd).reshape(EXT_R, WINC, 128)
        return carry

    lax.fori_loop(0, TW // BW, block, 0)

    back_src = [gns_s.at[0], gns_s.at[1], gew_s.at[0], gew_s.at[1]] + [gdg_s.at[i] for i in range(4)]
    back_dst = [gns_r.at[0], gns_r.at[1], gew_r.at[0], gew_r.at[1]] + [gdg_r.at[i] for i in range(4)]
    back = [halo_copy(way, back_src, back_dst, b_ss, b_rs) for way in range(8)]
    for way in range(8):
        dlat, dlon = WAYS[way]
        rows = {-1: slice(0, RAD), 1: slice(RAD + TH, EXT_R), 0: body}[dlat]
        cols = {-1: slice(0, PAD), 1: slice(PAD + TW, EXT_C), 0: slice(PAD, PAD + TW)}[dlon]
        flat = (rows.stop - rows.start) * (cols.stop - cols.start)

        def give(way=way, rows=rows, cols=cols, flat=flat):
            back_src[way][...] = gx[rows, cols, :].reshape(flat, 2 * WID).astype(BF16)
            back[way].start()

        when(can_send, way, give)

    def e_chunk(chunk):
        dq = dq_s[...].reshape(ROWS, WID)
        oo = o_s[...].reshape(ROWS, WID)
        return jnp.concatenate([mm(xt[chunk], dq), mm(gt[chunk], oo)], axis=1)

    def e_copy(k):
        return rcopy(e_s.at[k], e_r.at[k], e_ss.at[k], e_rs.at[k], tile(0, k + 1), h)

    def l_copy(k):
        return rcopy(l_s.at[k], l_r.at[k], l_ss.at[k], l_rs.at[k], tile(0, k + 1), h)

    def e_step(k, carry):
        e_s[k] = e_chunk(lax.rem(lon + k + 1, LON)).astype(BF16)
        e_copy(k).start()
        return carry

    lax.fori_loop(0, LON - 1, e_step, 0)
    own_e[...] = e_chunk(lon)

    for s in range(4):
        tacc[s] = mm(dq_s[...].reshape(ROWS, WID), w_v[0, s], 1, 1)

    for way in range(8):
        dlat, dlon = WAYS[way]
        rows = {-1: slice(TH, RAD + TH), 1: slice(RAD, 2 * RAD), 0: body}[dlat]
        cols = {-1: slice(TW, TW + PAD), 1: slice(PAD, 2 * PAD), 0: slice(PAD, PAD + TW)}[dlon]
        shape = shape_of(rows, cols)

        def fold(way=way, rows=rows, cols=cols, shape=shape):
            back[way].wait_recv()
            gx[rows, cols, :] += back_dst[way][...].astype(F32).reshape(shape)

        when(can_recv, way, fold)

    def round_g(i, carry):
        rows = pl.ds(pl.multiple_of(i * TW, TW), TW)
        dkv[rows, :] = gx[i + RAD, PAD : PAD + TW, :].astype(BF16)
        return carry

    lax.fori_loop(0, TH, round_g, 0)

    def l_step(k, carry):
        l_s[k] = mm(xt[lax.rem(lon + k + 1, LON)], dkv[...]).astype(BF16)
        l_copy(k).start()
        return carry

    lax.fori_loop(0, LON - 1, l_step, 0)
    own_l[...] = mm(xt[lon], dkv[...])

    def t_full(s):
        return (
            tacc[s]
            + mm(dkv[:, 0:WID], w_v[1, s], 1, 1)
            + mm(dkv[:, WID : 2 * WID], w_v[2, s], 1, 1)
        )

    t_opp = rcopy(t_s.at[0], t_r.at[0], t_ss.at[0], t_rs.at[0], g, sib)
    t_sib = rcopy(t_s.at[1], t_r.at[1], t_ss.at[1], t_rs.at[1], g, sib)
    t_far = rcopy(t_s.at[2], t_r.at[2], t_ss.at[2], t_rs.at[2], g, far)
    t_s[0] = t_full(opp).astype(BF16)
    t_opp.start()
    t_s[1] = t_full(sib).astype(BF16)
    t_sib.start()
    far_part = t_full(far)
    t_opp.wait_recv()
    t_s[2] = (far_part + t_r[0].astype(F32)).astype(BF16)
    t_far.start()
    tacc[h] = t_full(h)

    def e2_copy(k):
        to = lax.rem(lat + k + 1, LAT)
        rows = pl.ds(pl.multiple_of(to * 16, 16), 16)
        return rcopy(pe_b.at[rows], e2_r.at[k], e2_ss.at[k], e2_rs.at[k], tile(k + 1, 0), h)

    def l2_copy(k):
        to = lax.rem(lat + k + 1, LAT)
        rows = pl.ds(pl.multiple_of(to * 16, 16), 16)
        return rcopy(pl_b.at[rows], l2_r.at[k], l2_ss.at[k], l2_rs.at[k], tile(k + 1, 0), h)

    def level(own, first_copy, recv, packed, second_copy):
        def add(k, carry):
            first_copy(k).wait_recv()
            own[...] += recv[k].astype(F32)
            return carry

        lax.fori_loop(0, LON - 1, add, 0)
        packed[...] = own[...].astype(BF16)

        def send(k, carry):
            second_copy(k).start()
            return carry

        lax.fori_loop(0, LAT - 1, send, 0)

    level(own_e, e_copy, e_r, pe_b, e2_copy)
    level(own_l, l_copy, l_r, pl_b, l2_copy)

    t_sib.wait_recv()
    t_far.wait_recv()
    tok_ref[...] = (tacc[h] + t_r[1].astype(F32) + t_r[2].astype(F32)).astype(BF16)

    def finish(out, own, second_copy, recv):
        out[...] = own[pl.ds(pl.multiple_of(lat * 16, 16), 16), :]

        def add(k, carry):
            second_copy(k).wait_recv()
            out[...] += recv[k].astype(F32)
            return carry

        lax.fori_loop(0, LAT - 1, add, 0)

    finish(eo_ref, own_e, e2_copy, e2_r)
    finish(lo_ref, own_l, l2_copy, l2_r)

    for copy in (x_sib, x_far, x_fwd, g_sib, g_far, g_fwd, t_opp, t_sib, t_far):
        copy.wait_send()
    for way in range(8):
        when(can_send, way, halo[way].wait_send)
        when(can_send, way, back[way].wait_send)

    def drain(k, carry):
        e_copy(k).wait_send()
        l_copy(k).wait_send()
        e2_copy(k).wait_send()
        l2_copy(k).wait_send()
        return carry

    lax.fori_loop(0, LON - 1, drain, 0)


def local(tokens, qkv_weight, out_weight, out_grad):
    vm = pltpu.VMEM
    dma = pltpu.SemaphoreType.DMA
    scratch = [
        vm((3, 4, WID, WID), BF16),
        vm((WID, 4 * WID), BF16),
        vm((3, ROWS, WID), BF16),
        vm((3, ROWS, WID), BF16),
        vm((ROWS, 2 * WID), F32),
        vm((ROWS, 2 * WID), BF16),
        vm((2, EDGE, 2 * WID), BF16),
        vm((2, SLAB, 2 * WID), BF16),
        vm((2, EDGE, 2 * WID), BF16),
        vm((4, CORNER, 2 * WID), BF16),
        vm((EXT_R, EXT_C, 2 * WID), F32),
        vm((EXT_R, EXT_C, 2 * WID), F32),
        vm((TH, TW, WID), BF16),
        vm((TH, TW, WID), BF16),
        vm((TH, TW, WID), BF16),
        vm((TH, TW, WID), BF16),
        vm((ROWS, 2 * WID), BF16),
        vm((KEYS, QN), F32),
        vm((LON, 128, ROWS), BF16),
        vm((LON, 128, ROWS), BF16),
        vm((2, SLAB, 2 * WID), BF16),
        vm((2, EDGE, 2 * WID), BF16),
        vm((4, CORNER, 2 * WID), BF16),
        vm((2, SLAB, 2 * WID), BF16),
        vm((2, EDGE, 2 * WID), BF16),
        vm((4, CORNER, 2 * WID), BF16),
        vm((LON - 1, 128, 2 * WID), BF16),
        vm((LON - 1, 128, 2 * WID), BF16),
        vm((LON - 1, 128, 2 * WID), BF16),
        vm((LON - 1, 128, 2 * WID), BF16),
        vm((128, 2 * WID), F32),
        vm((128, 2 * WID), F32),
        vm((128, 2 * WID), BF16),
        vm((128, 2 * WID), BF16),
        vm((LAT - 1, 16, 2 * WID), BF16),
        vm((LAT - 1, 16, 2 * WID), BF16),
        vm((4, ROWS, WID), F32),
        vm((3, ROWS, WID), BF16),
        vm((3, ROWS, WID), BF16),
        dma((2,)),
        dma((6,)), dma((6,)),
        dma((8,)), dma((8,)),
        dma((8,)), dma((8,)),
        dma((7,)), dma((7,)),
        dma((7,)), dma((7,)),
        dma((7,)), dma((7,)),
        dma((7,)), dma((7,)),
        dma((3,)), dma((3,)),
    ]
    in_vmem = pl.BlockSpec(memory_space=pltpu.VMEM)
    anywhere = pl.BlockSpec(memory_space=pl.ANY)
    d_tok, early, late = pl.pallas_call(
        kernel,
        out_shape=(
            jax.ShapeDtypeStruct((ROWS, WID), BF16),
            jax.ShapeDtypeStruct((16, 2 * WID), F32),
            jax.ShapeDtypeStruct((16, 2 * WID), F32),
        ),
        in_specs=[in_vmem, in_vmem, anywhere, anywhere],
        out_specs=(in_vmem, in_vmem, in_vmem),
        scratch_shapes=scratch,
        compiler_params=pltpu.CompilerParams(
            collective_id=0, has_side_effects=True, vmem_limit_bytes=56 * 1024 * 1024
        ),
        cost_estimate=pl.CostEstimate(flops=8_000_000_000, bytes_accessed=4_000_000, transcendentals=1_400_000),
    )(
        tokens.reshape(ROWS, WID),
        out_grad.reshape(ROWS, WID),
        qkv_weight.reshape(3, 4, WID, WID),
        out_weight,
    )
    d_qkv = jnp.stack([early[:, :WID], late[:, :WID], late[:, WID:]])
    return d_tok.reshape(tokens.shape), d_qkv, early[:, WID:].T


def solution(mesh):
    in_specs = (
        P("grid", None, None, "heads"),
        P(None, None, "heads"),
        P("heads", None),
        P("grid", None, None, "heads"),
    )
    out_specs = (P("grid", None, None, "heads"), P(None, "grid", "heads"), P("heads", "grid"))
    return jax.shard_map(local, mesh=mesh, in_specs=in_specs, out_specs=out_specs, check_vma=False)
```

time: 1390 us -> 87.3 us (0.06)
  waiting for transfers between devices: 1180 us -> 0 us
  local copies, waits for them, and re-layouts: 126 us -> 3.75 us
  Pallas kernels: 0 us -> 82 us
  matrix products: 25 us -> 0 us
  other arithmetic: 19.3 us -> 0.62 us
  starting transfers between devices: 16.1 us -> 0 us
  between operations: 14.9 us -> 0.64 us
    unnamed x6 -> x0, waiting for transfers between devices: 693 us -> none
    reduce_scatter x2 -> x0, waiting for transfers between devices: 395 us -> none  [the longest x1 367 us: local(): lax.psum_scatter(out_term, 'grid', scatter_dimension=1, tiled=True)]
    pallas_call x0 -> x1, Pallas kernels: none -> 82 us  [local(): pl.pallas_call(kernel, out_shape=(jax.ShapeDtypeStruct((ROWS, WID), BF16)...]
    all_gather x2 -> x0, waiting for transfers between devices: 50.1 us -> none  [the longest x1 26.7 us: local(): lax.all_gather(tokens, 'heads', axis=3, tiled=True)]
    ppermute x8 -> x0, waiting for transfers between devices: 45.5 us -> none  [from_behind(): return lax.ppermute(value, axis, pairs)]
    scatter-add x9 -> x0, local copies, waits for them, and re-layouts: 40.2 us -> none  [the longest x7 36.9 us: band_step(): band_grads = band_grads.at[:, block_col * band_rows:block_col * band_rows...]
    reshape x6 -> x0, local copies, waits for them, and re-layouts: 33.8 us -> none  [the longest x2 16 us: band_step(): d_value.reshape(block_count, window, window, local_width)]
    dot_general x11 -> x0, matrix products: 25 us -> none  [the longest x1 3.91 us: local(): jnp.einsum('nd,cne->cde', token_rows, d_proj, preferred_element_type=jnp....]
  transfers between devices with their start and end apart: 13 -> 0, of which waited for: 11 -> 0; matrix products, arithmetic and copies ran while one was open for 2% -> 0% of each run, Pallas kernels for 0% -> 0%
where the time goes in v1:
time: 87.3 us; the launch traced here: 87 us
  Pallas kernels  82 us (94%)
  local copies, waits for them, and re-layouts  3.75 us (4%)
    pallas_call x1, Pallas kernels, local(): pl.pallas_call(kernel, out_shape=(jax.ShapeDtypeStruct((ROWS, WID), BF16)...  82 us

profile of v1, /device:TPU:2, one launch (start us, length us, event | category | flops | bytes accessed | tf_op | source)
XLA Modules:
  0.0 87.0 jit_solution(2990606885889356674)
XLA Ops:
  0.6 82.0 %shard_map.67 = (bf16[512,256]{1,0:T(8,128)(2,1)}, f32[16,512]{1,0:T(8,128)}, f32[16,512]{1,0:T(8,128)}) custom-call(bf16[512,256]{1,0:T(8,128)(2,1)} %bitcast.14, bf16[512,256]{1,0:T(8,128)(2,1)} %bitcast.15, bf16[3,4,256,256]{3,2,1,0:T(8,128)(2,1)} %bitcast.13, bf16[256,1024]{1,0:T(8,128)(2,1)} %wo_any.1), custom_call_target="tpu_custom_call" | custom-call | flops 8000000000 | bytes 4000000 | tf_op jit(solution)/shard_map/pallas_call | solution.py:471
  82.6 1.3 %slice_bitcast_fusion = (f32[256,16]{0,1:T(8,128)}, f32[1,16,256]{2,1,0:T(8,128)S(1)}) fusion(f32[16,512]{1,0:T(8,128)} %get-tuple-element.7), kind=kLoop, calls=%fused_computation.1 | loop fusion | bytes 65536 | tf_op jit(solution)/shard_map/transpose | solution.py:492
  84.0 0.7 slice_bitcast_fusion.2
  84.7 0.6 pad_maximum_fusion
  85.3 1.7 %copy.8 = bf16[1,8,64,256]{3,2,1,0:T(8,128)(2,1)} copy(bf16[1,8,64,256]{3,2,1,0:T(8,128)(2,1)} %bitcast.12) | data formatting | bytes 524288

commit v2 on v1

v2 whole, which is shorter than its diff:
```python
import jax
import jax.numpy as jnp
from jax import lax
from jax.experimental import pallas as pl
from jax.experimental.pallas import tpu as pltpu
from jax.sharding import PartitionSpec as P

MESH = pl.DeviceIdType.MESH
F32 = jnp.float32
BF16 = jnp.bfloat16

HD = 64
RAD = 6
LON = 8
LAT = 8
TH = 8
TW = 64
WID = 256
ROWS = TH * TW
EXT_R = TH + 2 * RAD
PAD = 8
EXT_C = TW + 2 * PAD
BW = 16
WINC = BW + 2 * PAD
KEYS = EXT_R * WINC
QN = TH * BW
NB = TW // BW
SLAB = RAD * BW
EDGE = TH * PAD
CORNER = RAD * PAD
PIECES = EXT_C // BW
ORDER = (0, 3, 1, 2)


def mm(a, b, ca=1, cb=0):
    return lax.dot_general(a, b, (((ca,), (cb,)), ((), ())), preferred_element_type=F32)


def kernel(
    x_ref, g_ref, w_any, wo_any,
    tok_ref, eo_ref, lo_ref,
    w_v, wo_v, xf, gf, kvb, edge, ns_r, ew_r, co_r, kvx, gx,
    q_s, do_s, o_s, dq_s, dkv, bias, xt, gt,
    gns_s, gew_s, gns_r, gew_r,
    e_s, e_r, l_s, l_r, own_e, own_l, pe_b, pl_b, e2_r, l2_r,
    tacc, t_s, t_r,
    w_sem, x_ss, x_rs, g_ss, g_rs, n_ss, n_rs, s_ss, s_rs, ew_ss, ew_rs, co_ss, co_rs,
    bn_ss, bn_rs, bs_ss, bs_rs, be_ss, be_rs,
    e_ss, e_rs, l_ss, l_rs, e2_ss, e2_rs, l2_ss, l2_rs, t_ss, t_rs,
):
    g = lax.axis_index("grid")
    h = lax.axis_index("heads")
    lat = lax.rem(g, LAT)
    lon = lax.div(g, LAT)
    sib = h + 1 - 2 * lax.rem(h, 2)
    far = h + 2 - 4 * lax.div(h, 2)
    opp = 3 - h
    slots = (h, sib, far, opp)

    w_copy = pltpu.make_async_copy(w_any, w_v, w_sem.at[0])
    wo_copy = pltpu.make_async_copy(wo_any, wo_v, w_sem.at[1])
    w_copy.start()
    wo_copy.start()

    def tile(dlat, dlon):
        return lax.rem(lon + dlon + LON, LON) * LAT + lax.rem(lat + dlat + LAT, LAT)

    has_n = lat > 0
    has_s = lat < LAT - 1
    can_send = (has_n, has_s)
    can_recv = (has_s, has_n)
    step = (-1, 1)

    bar = pltpu.get_barrier_semaphore()

    def greet(to_grid, to_head):
        pl.semaphore_signal(bar, inc=1, device_id=(to_grid, to_head), device_id_type=MESH)

    greet(g, sib)
    greet(g, far)
    for k in range(1, 8):
        greet(tile(k, 0), h)
        greet(tile(0, k), h)
    pl.semaphore_wait(bar, 16)

    def rcopy(src, dst, ss, rs, to_grid, to_head):
        return pltpu.make_async_remote_copy(
            src_ref=src, dst_ref=dst, send_sem=ss, recv_sem=rs,
            device_id=(to_grid, to_head), device_id_type=MESH,
        )

    def gather(src, full, ss, rs, c):
        mine = src.at[:, c * BW : (c + 1) * BW, :]
        return (
            rcopy(mine, full.at[0, c], ss.at[c], rs.at[c], g, sib),
            rcopy(mine, full.at[1, c], ss.at[NB + c], rs.at[NB + c], g, far),
            rcopy(full.at[1, c], full.at[2, c], ss.at[2 * NB + c], rs.at[2 * NB + c], g, sib),
        )

    x_copies = [gather(x_ref, xf, x_ss, x_rs, c) for c in range(NB)]
    g_copies = [gather(g_ref, gf, g_ss, g_rs, c) for c in range(NB)]
    for c in ORDER:
        x_copies[c][1].start()
        x_copies[c][0].start()

    def chunk_of(ref, full, k, c):
        value = ref[:, c * BW : (c + 1) * BW, :] if k == 0 else full[k - 1, c]
        return value.reshape(QN, WID)

    key = lax.broadcasted_iota(jnp.int32, (KEYS, QN), 0)
    qry = lax.broadcasted_iota(jnp.int32, (KEYS, QN), 1)
    key_r, key_c = lax.div(key, WINC), lax.rem(key, WINC)
    dr = key_r - lax.div(qry, BW)
    dc = key_c - lax.rem(qry, BW)
    at_lat = key_r + (lat * TH - RAD)
    fine = (dr >= 0) & (dr <= 2 * RAD) & (dc >= PAD - RAD) & (dc <= PAD + RAD)
    fine = fine & (at_lat >= 0) & (at_lat < LAT * TH)
    bias[...] = jnp.where(fine, 0.0, -1e30)

    def clear(i, carry):
        gx[i] = jnp.zeros((EXT_C, 2 * WID), F32)
        return carry

    lax.fori_loop(0, EXT_R, clear, 0)
    body = slice(RAD, RAD + TH)
    rim = (slice(RAD + TH, EXT_R), slice(0, RAD))
    for way in range(2):

        def blank(way=way):
            kvx[rim[way], :, :] = jnp.zeros((RAD, EXT_C, 2 * WID), F32)

        pl.when(jnp.logical_not(can_recv[way]))(blank)
    w_copy.wait()

    def ns_copy(way, c):
        rows = slice(0, SLAB) if way == 0 else slice(QN - SLAB, QN)
        ss, rs = (n_ss, n_rs) if way == 0 else (s_ss, s_rs)
        return rcopy(kvb.at[c, rows], ns_r.at[way, c], ss.at[c], rs.at[c], tile(step[way], 0), h)

    def ew_copy(way):
        return rcopy(edge.at[way], ew_r.at[way], ew_ss.at[way], ew_rs.at[way], tile(0, step[way]), h)

    def corner_copy(way, side):
        rows = slice(0, CORNER) if way == 0 else slice(EDGE - CORNER, EDGE)
        at = 2 * way + side
        return rcopy(ew_r.at[side, rows], co_r.at[at], co_ss.at[at], co_rs.at[at], tile(step[way], 0), h)

    for c in ORDER:
        total = [None, None]

        def add_kv(k, c=c, total=total):
            block = chunk_of(x_ref, xf, k, c)
            for i in range(2):
                part = mm(block, w_v[i + 1, slots[k]])
                total[i] = part if total[i] is None else total[i] + part

        add_kv(0)
        x_copies[c][0].wait_recv()
        add_kv(1)
        x_copies[c][1].wait_recv()
        x_copies[c][2].start()
        if c == ORDER[-1]:
            for other in ORDER:
                g_copies[other][1].start()
                g_copies[other][0].start()
        add_kv(2)
        x_copies[c][2].wait_recv()
        add_kv(3)
        value = jnp.concatenate([total[0].astype(BF16), total[1].astype(BF16)], axis=1)
        kvb[c] = value
        for way in range(2):
            pl.when(can_send[way])(ns_copy(way, c).start)
        wide = value.astype(F32).reshape(TH, BW, 2 * WID)
        kvx[body, PAD + c * BW : PAD + (c + 1) * BW, :] = wide
        if c == 0:
            edge[0] = wide[:, :PAD, :].reshape(EDGE, 2 * WID).astype(BF16)
            ew_copy(0).start()
        if c == NB - 1:
            edge[1] = wide[:, BW - PAD :, :].reshape(EDGE, 2 * WID).astype(BF16)
            ew_copy(1).start()

    def turn(ref, full, out, c):
        for k in range(4):
            piece = chunk_of(ref, full, k, c)
            for j in range(2):
                part = piece[:, j * 128 : (j + 1) * 128].astype(F32)
                out[2 * slots[k] + j, :, c * QN : (c + 1) * QN] = part.T.astype(BF16)

    def query(c):
        total = mm(chunk_of(x_ref, xf, 0, c), w_v[0, slots[0]])
        for k in range(1, 4):
            total += mm(chunk_of(x_ref, xf, k, c), w_v[0, slots[k]])
        q_s[c] = total.astype(BF16) * jnp.asarray(HD**-0.5, BF16)

    for c in ORDER[:2]:
        query(c)
    for side in range(2):
        ew_copy(side).wait_recv()
        for way in range(2):
            pl.when(can_send[way])(corner_copy(way, side).start)
    for c in ORDER[2:]:
        query(c)
    for c in range(NB):
        turn(x_ref, xf, xt, c)
    for side in range(2):
        cols = slice(PAD + TW, EXT_C) if side == 0 else slice(0, PAD)
        kvx[body, cols, :] = ew_r[side].astype(F32).reshape(TH, PAD, 2 * WID)

    wo_copy.wait()
    for c in ORDER:
        g_copies[c][0].wait_recv()
        g_copies[c][1].wait_recv()
        g_copies[c][2].start()
        total = None
        for k in range(4):
            if k == 3:
                g_copies[c][2].wait_recv()
            cols = pl.ds(pl.multiple_of(slots[k] * WID, WID), WID)
            part = mm(chunk_of(g_ref, gf, k, c), wo_v[:, cols], 1, 1)
            total = part if total is None else total + part
        do_s[c] = total.astype(BF16)
        turn(g_ref, gf, gt, c)

    def take_chunk(c):
        for way in range(2):

            def take(way=way):
                ns_copy(way, c).wait_recv()
                value = ns_r[way, c].astype(F32).reshape(RAD, BW, 2 * WID)
                kvx[rim[way], PAD + c * BW : PAD + (c + 1) * BW, :] = value

            pl.when(can_recv[way])(take)

    def take_corners(side):
        cols = slice(PAD + TW, EXT_C) if side == 0 else slice(0, PAD)
        for way in range(2):

            def take(way=way):
                corner_copy(way, side).wait_recv()
                kvx[rim[way], cols, :] = co_r[2 * way + side].astype(F32).reshape(RAD, PAD, 2 * WID)

            pl.when(can_recv[way])(take)

    lane = lax.broadcasted_iota(jnp.int32, (QN, 128), 1)
    first = lane < HD

    def two_heads(value):
        zero = jnp.zeros_like(value)
        return jnp.concatenate([jnp.where(first, value, zero), jnp.where(first, zero, value)], axis=0)

    def untwo(value):
        picked = jnp.concatenate([value[:HD, :QN], value[HD:, QN:]], axis=0)
        return picked.T.astype(BF16)

    def block(b):
        window = slice(b * BW, b * BW + WINC)
        for p in range(2):
            cols = slice(p * 128, (p + 1) * 128)
            vcols = slice(WID + p * 128, WID + (p + 1) * 128)
            keys = kvx[:, window, cols].reshape(KEYS, 128).astype(BF16)
            vals = kvx[:, window, vcols].reshape(KEYS, 128).astype(BF16)
            qq = two_heads(q_s[b, :, cols])
            dd = two_heads(do_s[b, :, cols])
            scores = mm(keys, qq, 1, 1)
            b1 = bias[...]
            raw = jnp.exp(scores + jnp.concatenate([b1, b1], axis=1))
            prob = raw * (1.0 / jnp.sum(raw, axis=0, keepdims=True))
            prob_b = prob.astype(BF16)
            d_prob = mm(vals, dd, 1, 1)
            delta = jnp.sum(prob * d_prob, axis=0, keepdims=True)
            d_sc = (prob * (d_prob - delta)).astype(BF16)
            o_s[b, :, cols] = untwo(mm(vals, prob_b, 0, 0))
            dq_s[b, :, cols] = untwo(mm(keys, d_sc, 0, 0) * HD**-0.5)
            gx[:, window, cols] += mm(d_sc, qq).reshape(EXT_R, WINC, 128)
            gx[:, window, vcols] += mm(prob_b, dd).reshape(EXT_R, WINC, 128)

    def back_copy(way, p):
        ss, rs = (bn_ss, bn_rs) if way == 0 else (bs_ss, bs_rs)
        return rcopy(gns_s.at[way, p], gns_r.at[way, p], ss.at[p], rs.at[p], tile(step[way], 0), h)

    def back_ew(way):
        return rcopy(gew_s.at[way], gew_r.at[way], be_ss.at[way], be_rs.at[way], tile(0, step[way]), h)

    def give(p):
        for way in range(2):
            rows = slice(0, RAD) if way == 0 else slice(RAD + TH, EXT_R)

            def send(way=way, rows=rows):
                value = gx[rows, p * BW : (p + 1) * BW, :].reshape(SLAB, 2 * WID)
                gns_s[way, p] = value.astype(BF16)
                back_copy(way, p).start()

            pl.when(can_send[way])(send)

    def fold(p):
        for way in range(2):
            rows = slice(TH, RAD + TH) if way == 0 else slice(RAD, 2 * RAD)

            def add(way=way, rows=rows):
                back_copy(way, p).wait_recv()
                value = gns_r[way, p].astype(F32).reshape(RAD, BW, 2 * WID)
                gx[rows, p * BW : (p + 1) * BW, :] += value

            pl.when(can_recv[way])(add)

    def give_ew(way):
        cols = slice(0, PAD) if way == 0 else slice(PAD + TW, EXT_C)
        gew_s[way] = gx[body, cols, :].reshape(EDGE, 2 * WID).astype(BF16)
        back_ew(way).start()

    def fold_ew(way):
        cols = slice(TW, TW + PAD) if way == 0 else slice(PAD, 2 * PAD)
        back_ew(way).wait_recv()
        gx[body, cols, :] += gew_r[way].astype(F32).reshape(TH, PAD, 2 * WID)

    for c in ORDER:
        if c != 3:
            take_chunk(c)
    block(1)
    take_corners(1)
    block(0)
    give(0)
    give(1)
    take_chunk(3)
    take_corners(0)
    block(3)
    give(4)
    block(2)
    give(2)
    give(3)

    def e_chunk(chunk):
        dq = dq_s[...].reshape(ROWS, WID)
        oo = o_s[...].reshape(ROWS, WID)
        return jnp.concatenate([mm(xt[chunk], dq), mm(gt[chunk], oo)], axis=1)

    def e_copy(k):
        return rcopy(e_s.at[k], e_r.at[k], e_ss.at[k], e_rs.at[k], tile(0, k + 1), h)

    def l_copy(k):
        return rcopy(l_s.at[k], l_r.at[k], l_ss.at[k], l_rs.at[k], tile(0, k + 1), h)

    def e_step(k, carry):
        e_s[k] = e_chunk(lax.rem(lon + k + 1, LON)).astype(BF16)
        e_copy(k).start()
        return carry

    lax.fori_loop(0, LON - 1, e_step, 0)
    own_e[...] = e_chunk(lon)
    fold(0)
    give_ew(0)
    fold(4)
    give_ew(1)

    for s in range(4):
        tacc[s] = mm(dq_s[...].reshape(ROWS, WID), w_v[0, s], 1, 1)

    for p in (1, 2, 3):
        fold(p)
    for way in range(2):
        fold_ew(way)
    for c in range(NB):
        value = gx[body, PAD + c * BW : PAD + (c + 1) * BW, :].reshape(QN, 2 * WID)
        dkv[c * QN : (c + 1) * QN, :] = value.astype(BF16)

    def l_step(k, carry):
        l_s[k] = mm(xt[lax.rem(lon + k + 1, LON)], dkv[...]).astype(BF16)
        l_copy(k).start()
        return carry

    lax.fori_loop(0, LON - 1, l_step, 0)
    own_l[...] = mm(xt[lon], dkv[...])

    def t_full(s):
        return (
            tacc[s]
            + mm(dkv[:, 0:WID], w_v[1, s], 1, 1)
            + mm(dkv[:, WID : 2 * WID], w_v[2, s], 1, 1)
        )

    t_opp = rcopy(t_s.at[0], t_r.at[0], t_ss.at[0], t_rs.at[0], g, sib)
    t_sib = rcopy(t_s.at[1], t_r.at[1], t_ss.at[1], t_rs.at[1], g, sib)
    t_far = rcopy(t_s.at[2], t_r.at[2], t_ss.at[2], t_rs.at[2], g, far)
    t_s[0] = t_full(opp).astype(BF16)
    t_opp.start()
    t_s[1] = t_full(sib).astype(BF16)
    t_sib.start()
    far_part = t_full(far)
    t_opp.wait_recv()
    t_s[2] = (far_part + t_r[0].astype(F32)).astype(BF16)
    t_far.start()
    tacc[h] = t_full(h)

    def e2_copy(k):
        to = lax.rem(lat + k + 1, LAT)
        rows = pl.ds(pl.multiple_of(to * 16, 16), 16)
        return rcopy(pe_b.at[rows], e2_r.at[k], e2_ss.at[k], e2_rs.at[k], tile(k + 1, 0), h)

    def l2_copy(k):
        to = lax.rem(lat + k + 1, LAT)
        rows = pl.ds(pl.multiple_of(to * 16, 16), 16)
        return rcopy(pl_b.at[rows], l2_r.at[k], l2_ss.at[k], l2_rs.at[k], tile(k + 1, 0), h)

    def level(own, first_copy, recv, packed, second_copy):
        def add(k, carry):
            first_copy(k).wait_recv()
            own[...] += recv[k].astype(F32)
            return carry

        lax.fori_loop(0, LON - 1, add, 0)
        packed[...] = own[...].astype(BF16)

        def send(k, carry):
            second_copy(k).start()
            return carry

        lax.fori_loop(0, LAT - 1, send, 0)

    level(own_e, e_copy, e_r, pe_b, e2_copy)
    level(own_l, l_copy, l_r, pl_b, l2_copy)

    t_sib.wait_recv()
    t_far.wait_recv()
    for c in range(NB):
        rows = slice(c * QN, (c + 1) * QN)
        total = tacc[h, rows] + t_r[1, rows].astype(F32) + t_r[2, rows].astype(F32)
        tok_ref[:, c * BW : (c + 1) * BW, :] = total.astype(BF16).reshape(TH, BW, WID)

    def finish(out, own, second_copy, recv):
        out[...] = own[pl.ds(pl.multiple_of(lat * 16, 16), 16), :]

        def add(k, carry):
            second_copy(k).wait_recv()
            out[...] += recv[k].astype(F32)
            return carry

        lax.fori_loop(0, LAT - 1, add, 0)

    finish(eo_ref, own_e, e2_copy, e2_r)
    finish(lo_ref, own_l, l2_copy, l2_r)

    for copies in x_copies + g_copies + [(t_opp, t_sib, t_far)]:
        for copy in copies:
            copy.wait_send()
    for way in range(2):
        ew_copy(way).wait_send()
        back_ew(way).wait_send()

        def sent(way=way):
            for c in range(NB):
                ns_copy(way, c).wait_send()
            for side in range(2):
                corner_copy(way, side).wait_send()
            for p in range(PIECES):
                back_copy(way, p).wait_send()

        pl.when(can_send[way])(sent)

    def drain(k, carry):
        e_copy(k).wait_send()
        l_copy(k).wait_send()
        e2_copy(k).wait_send()
        l2_copy(k).wait_send()
        return carry

    lax.fori_loop(0, LON - 1, drain, 0)


def local(tokens, qkv_weight, out_weight, out_grad):
    vm = pltpu.VMEM
    dma = pltpu.SemaphoreType.DMA
    scratch = [
        vm((3, 4, WID, WID), BF16),
        vm((WID, 4 * WID), BF16),
        vm((3, NB, TH, BW, WID), BF16),
        vm((3, NB, TH, BW, WID), BF16),
        vm((NB, QN, 2 * WID), BF16),
        vm((2, EDGE, 2 * WID), BF16),
        vm((2, NB, SLAB, 2 * WID), BF16),
        vm((2, EDGE, 2 * WID), BF16),
        vm((4, CORNER, 2 * WID), BF16),
        vm((EXT_R, EXT_C, 2 * WID), F32),
        vm((EXT_R, EXT_C, 2 * WID), F32),
        vm((NB, QN, WID), BF16),
        vm((NB, QN, WID), BF16),
        vm((NB, QN, WID), BF16),
        vm((NB, QN, WID), BF16),
        vm((ROWS, 2 * WID), BF16),
        vm((KEYS, QN), F32),
        vm((LON, 128, ROWS), BF16),
        vm((LON, 128, ROWS), BF16),
        vm((2, PIECES, SLAB, 2 * WID), BF16),
        vm((2, EDGE, 2 * WID), BF16),
        vm((2, PIECES, SLAB, 2 * WID), BF16),
        vm((2, EDGE, 2 * WID), BF16),
        vm((LON - 1, 128, 2 * WID), BF16),
        vm((LON - 1, 128, 2 * WID), BF16),
        vm((LON - 1, 128, 2 * WID), BF16),
        vm((LON - 1, 128, 2 * WID), BF16),
        vm((128, 2 * WID), F32),
        vm((128, 2 * WID), F32),
        vm((128, 2 * WID), BF16),
        vm((128, 2 * WID), BF16),
        vm((LAT - 1, 16, 2 * WID), BF16),
        vm((LAT - 1, 16, 2 * WID), BF16),
        vm((4, ROWS, WID), F32),
        vm((3, ROWS, WID), BF16),
        vm((3, ROWS, WID), BF16),
        dma((2,)),
        dma((3 * NB,)), dma((3 * NB,)),
        dma((3 * NB,)), dma((3 * NB,)),
        dma((NB,)), dma((NB,)),
        dma((NB,)), dma((NB,)),
        dma((2,)), dma((2,)),
        dma((4,)), dma((4,)),
        dma((PIECES,)), dma((PIECES,)),
        dma((PIECES,)), dma((PIECES,)),
        dma((2,)), dma((2,)),
        dma((7,)), dma((7,)),
        dma((7,)), dma((7,)),
        dma((7,)), dma((7,)),
        dma((7,)), dma((7,)),
        dma((3,)), dma((3,)),
    ]
    in_vmem = pl.BlockSpec(memory_space=pltpu.VMEM)
    anywhere = pl.BlockSpec(memory_space=pl.ANY)
    d_tok, early, late = pl.pallas_call(
        kernel,
        out_shape=(
            jax.ShapeDtypeStruct((TH, TW, WID), BF16),
            jax.ShapeDtypeStruct((16, 2 * WID), F32),
            jax.ShapeDtypeStruct((16, 2 * WID), F32),
        ),
        in_specs=[in_vmem, in_vmem, anywhere, anywhere],
        out_specs=(in_vmem, in_vmem, in_vmem),
        scratch_shapes=scratch,
        compiler_params=pltpu.CompilerParams(
            collective_id=0, has_side_effects=True, vmem_limit_bytes=56 * 1024 * 1024
        ),
        cost_estimate=pl.CostEstimate(flops=8_000_000_000, bytes_accessed=4_000_000, transcendentals=1_400_000),
    )(
        tokens.reshape(TH, TW, WID),
        out_grad.reshape(TH, TW, WID),
        qkv_weight.reshape(3, 4, WID, WID),
        out_weight,
    )
    d_qkv = jnp.stack([early[:, :WID], late[:, :WID], late[:, WID:]])
    return d_tok.reshape(tokens.shape), d_qkv, early[:, WID:].T


def solution(mesh):
    in_specs = (
        P("grid", None, None, "heads"),
        P(None, None, "heads"),
        P("heads", None),
        P("grid", None, None, "heads"),
    )
    out_specs = (P("grid", None, None, "heads"), P(None, "grid", "heads"), P("heads", "grid"))
    return jax.shard_map(local, mesh=mesh, in_specs=in_specs, out_specs=out_specs, check_vma=False)
```

time: 87.3 us -> 79.9 us (0.915)
  Pallas kernels: 82 us -> 74.6 us
    pallas_call x1, Pallas kernels: 82 us -> 74.6 us  [local(): pl.pallas_call(kernel, out_shape=(jax.ShapeDtypeStruct((TH, TW, WID), BF1...]
where the time goes in v2:
time: 79.9 us; the launch traced here: 79.6 us
  Pallas kernels  74.6 us (93%)
  local copies, waits for them, and re-layouts  3.75 us (5%)
    pallas_call x1, Pallas kernels, local(): pl.pallas_call(kernel, out_shape=(jax.ShapeDtypeStruct((TH, TW, WID), BF1...  74.6 us
    unnamed x1, local copies, waits for them, and re-layouts  1.67 us

profile of v2, /device:TPU:2, one launch (start us, length us, event | category | flops | bytes accessed | tf_op | source)
XLA Modules:
  0.0 79.6 jit_solution(5381963862483569851)
XLA Ops:
  0.6 74.6 %shard_map.67 = (bf16[8,64,256]{2,1,0:T(8,128)(2,1)}, f32[16,512]{1,0:T(8,128)}, f32[16,512]{1,0:T(8,128)}) custom-call(bf16[8,64,256]{2,1,0:T(8,128)(2,1)} %bitcast.14, bf16[8,64,256]{2,1,0:T(8,128)(2,1)} %bitcast.15, bf16[3,4,256,256]{3,2,1,0:T(8,128)(2,1)} %bitcast.13, bf16[256,1024]{1,0:T(8,128)(2,1)} %wo_any.1), custom_call_target="tpu_custom_call" | custom-call | flops 8000000000 | bytes 4000000 | tf_op jit(solution)/shard_map/pallas_call | solution.py:527
  75.3 1.3 %slice_bitcast_fusion = (f32[256,16]{0,1:T(8,128)}, f32[1,16,256]{2,1,0:T(8,128)S(1)}) fusion(f32[16,512]{1,0:T(8,128)} %get-tuple-element.7), kind=kLoop, calls=%fused_computation.1 | loop fusion | bytes 65536 | tf_op jit(solution)/shard_map/transpose | solution.py:548
  76.6 0.7 slice_bitcast_fusion.2
  77.3 0.6 pad_maximum_fusion
  78.0 1.7 %copy.8 = bf16[1,8,64,256]{3,2,1,0:T(8,128)(2,1)} copy(bf16[1,8,64,256]{3,2,1,0:T(8,128)(2,1)} %bitcast.12) | data formatting | bytes 524288

commit v3 on v2

--- a/solution.py
+++ b/solution.py
@@ -30,6 +30,8 @@
 CORNER = RAD * PAD
 PIECES = EXT_C // BW
 ORDER = (0, 3, 1, 2)
+BLOCKS = (1, 0, 3, 2)
+DIRECT = 384
 
 
 def mm(a, b, ca=1, cb=0):
@@ -38,15 +40,16 @@
 
 def kernel(
     x_ref, g_ref, w_any, wo_any,
-    tok_ref, eo_ref, lo_ref,
+    tok_ref, dqkv_ref, dwo_ref,
     w_v, wo_v, xf, gf, kvb, edge, ns_r, ew_r, co_r, kvx, gx,
     q_s, do_s, o_s, dq_s, dkv, bias, xt, gt,
     gns_s, gew_s, gns_r, gew_r,
     e_s, e_r, l_s, l_r, own_e, own_l, pe_b, pl_b, e2_r, l2_r,
+    m_s, m_f, m_r, own_m, pm_b, m2_r,
     tacc, t_s, t_r,
     w_sem, x_ss, x_rs, g_ss, g_rs, n_ss, n_rs, s_ss, s_rs, ew_ss, ew_rs, co_ss, co_rs,
     bn_ss, bn_rs, bs_ss, bs_rs, be_ss, be_rs,
-    e_ss, e_rs, l_ss, l_rs, e2_ss, e2_rs, l2_ss, l2_rs, t_ss, t_rs,
+    e_ss, e_rs, l_ss, l_rs, e2_ss, e2_rs, l2_ss, l2_rs, m_ss, m_rs, m2_ss, m2_rs, t_ss, t_rs,
 ):
     g = lax.axis_index("grid")
     h = lax.axis_index("heads")
@@ -145,6 +148,10 @@
         at = 2 * way + side
         return rcopy(ew_r.at[side, rows], co_r.at[at], co_ss.at[at], co_rs.at[at], tile(step[way], 0), h)
 
+    def arrive(copies, c):
+        copies[c][1].wait_recv()
+        copies[c][2].start()
+
     for c in ORDER:
         total = [None, None]
 
@@ -157,13 +164,15 @@
         add_kv(0)
         x_copies[c][0].wait_recv()
         add_kv(1)
-        x_copies[c][1].wait_recv()
-        x_copies[c][2].start()
-        if c == ORDER[-1]:
-            for other in ORDER:
+        if c == ORDER[0]:
+            arrive(x_copies, c)
+        add_kv(2)
+        if c != ORDER[-1]:
+            arrive(x_copies, ORDER[ORDER.index(c) + 1])
+        else:
+            for other in BLOCKS:
                 g_copies[other][1].start()
                 g_copies[other][0].start()
-        add_kv(2)
         x_copies[c][2].wait_recv()
         add_kv(3)
         value = jnp.concatenate([total[0].astype(BF16), total[1].astype(BF16)], axis=1)
@@ -207,13 +216,14 @@
         kvx[body, cols, :] = ew_r[side].astype(F32).reshape(TH, PAD, 2 * WID)
 
     wo_copy.wait()
-    for c in ORDER:
+
+    def cotangent(c, after):
         g_copies[c][0].wait_recv()
-        g_copies[c][1].wait_recv()
-        g_copies[c][2].start()
         total = None
         for k in range(4):
             if k == 3:
+                if after is not None:
+                    arrive(g_copies, after)
                 g_copies[c][2].wait_recv()
             cols = pl.ds(pl.multiple_of(slots[k] * WID, WID), WID)
             part = mm(chunk_of(g_ref, gf, k, c), wo_v[:, cols], 1, 1)
@@ -313,18 +323,22 @@
         back_ew(way).wait_recv()
         gx[body, cols, :] += gew_r[way].astype(F32).reshape(TH, PAD, 2 * WID)
 
-    for c in ORDER:
-        if c != 3:
-            take_chunk(c)
+    arrive(g_copies, 1)
+    cotangent(1, 0)
+    for c in (0, 1, 2):
+        take_chunk(c)
     block(1)
+    cotangent(0, 3)
     take_corners(1)
     block(0)
     give(0)
     give(1)
+    cotangent(3, 2)
     take_chunk(3)
     take_corners(0)
     block(3)
     give(4)
+    cotangent(2, None)
     block(2)
     give(2)
     give(3)
@@ -363,13 +377,27 @@
         value = gx[body, PAD + c * BW : PAD + (c + 1) * BW, :].reshape(QN, 2 * WID)
         dkv[c * QN : (c + 1) * QN, :] = value.astype(BF16)
 
+    def m_copy(k):
+        to = lax.rem(lat + k + 1, LAT)
+        rows = pl.ds(pl.multiple_of(to * 16, 16), 16)
+        return rcopy(m_s.at[:, rows], m_r.at[k], m_ss.at[k], m_rs.at[k], tile(k + 1, 0), h)
+
     def l_step(k, carry):
-        l_s[k] = mm(xt[lax.rem(lon + k + 1, LON)], dkv[...]).astype(BF16)
+        l_s[k] = mm(xt[lax.rem(lon + k + 1, LON)], dkv[:, :DIRECT]).astype(BF16)
         l_copy(k).start()
         return carry
 
+    def m_step(k, carry):
+        full = mm(xt[k], dkv[:, DIRECT:])
+        m_s[k] = full.astype(BF16)
+        m_f[k] = full
+        return carry
+
     lax.fori_loop(0, LON - 1, l_step, 0)
-    own_l[...] = mm(xt[lon], dkv[...])
+    lax.fori_loop(0, LON, m_step, 0)
+    for k in range(LAT - 1):
+        m_copy(k).start()
+    own_l[...] = mm(xt[lon], dkv[:, :DIRECT])
 
     def t_full(s):
         return (
@@ -416,7 +444,22 @@
 
         lax.fori_loop(0, LAT - 1, send, 0)
 
+    def m2_copy(k):
+        to = lax.rem(lon + k + 1, LON)
+        return rcopy(pm_b.at[to], m2_r.at[k], m2_ss.at[k], m2_rs.at[k], tile(0, k + 1), h)
+
     level(own_e, e_copy, e_r, pe_b, e2_copy)
+
+    here = pl.ds(pl.multiple_of(lat * 16, 16), 16)
+    total = m_f[:, here, :]
+    for k in range(LAT - 1):
+        m_copy(k).wait_recv()
+        total += m_r[k].astype(F32)
+    pm_b[...] = total.astype(BF16)
+    own_m[...] = total
+    for k in range(LON - 1):
+        m2_copy(k).start()
+
     level(own_l, l_copy, l_r, pl_b, l2_copy)
 
     t_sib.wait_recv()
@@ -426,18 +469,24 @@
         total = tacc[h, rows] + t_r[1, rows].astype(F32) + t_r[2, rows].astype(F32)
         tok_ref[:, c * BW : (c + 1) * BW, :] = total.astype(BF16).reshape(TH, BW, WID)
 
-    def finish(out, own, second_copy, recv):
-        out[...] = own[pl.ds(pl.multiple_of(lat * 16, 16), 16), :]
-
-        def add(k, carry):
+    def finish(own, second_copy, recv):
+        total = own[here, :]
+        for k in range(LAT - 1):
             second_copy(k).wait_recv()
-            out[...] += recv[k].astype(F32)
-            return carry
-
-        lax.fori_loop(0, LAT - 1, add, 0)
-
-    finish(eo_ref, own_e, e2_copy, e2_r)
-    finish(lo_ref, own_l, l2_copy, l2_r)
+            total += recv[k].astype(F32)
+        return total
+
+    early = finish(own_e, e2_copy, e2_r)
+    dqkv_ref[0] = early[:, :WID]
+    dwo_ref[...] = early[:, WID:]
+    last = own_m[lon]
+    for k in range(LON - 1):
+        m2_copy(k).wait_recv()
+        last += m2_r[k].astype(F32)
+    dqkv_ref[2, :, WID - 128 :] = last
+    late = finish(own_l, l2_copy, l2_r)
+    dqkv_ref[1] = late[:, :WID]
+    dqkv_ref[2, :, : WID - 128] = late[:, WID:]
 
     for copies in x_copies + g_copies + [(t_opp, t_sib, t_far)]:
         for copy in copies:
@@ -461,9 +510,17 @@
         l_copy(k).wait_send()
         e2_copy(k).wait_send()
         l2_copy(k).wait_send()
+        m_copy(k).wait_send()
+        m2_copy(k).wait_send()
         return carry
 
     lax.fori_loop(0, LON - 1, drain, 0)
+
+
+def hand_out(tok_in, dqkv_in, dwo_in, tok_ref, dqkv_ref, dwo_ref):
+    tok_ref[...] = tok_in[...]
+    dqkv_ref[...] = dqkv_in[...]
+    dwo_ref[...] = dwo_in[...]
 
 
 def local(tokens, qkv_weight, out_weight, out_grad):
@@ -495,14 +552,20 @@
         vm((2, EDGE, 2 * WID), BF16),
         vm((LON - 1, 128, 2 * WID), BF16),
         vm((LON - 1, 128, 2 * WID), BF16),
-        vm((LON - 1, 128, 2 * WID), BF16),
-        vm((LON - 1, 128, 2 * WID), BF16),
+        vm((LON - 1, 128, DIRECT), BF16),
+        vm((LON - 1, 128, DIRECT), BF16),
         vm((128, 2 * WID), F32),
-        vm((128, 2 * WID), F32),
+        vm((128, DIRECT), F32),
         vm((128, 2 * WID), BF16),
-        vm((128, 2 * WID), BF16),
+        vm((128, DIRECT), BF16),
         vm((LAT - 1, 16, 2 * WID), BF16),
-        vm((LAT - 1, 16, 2 * WID), BF16),
+        vm((LAT - 1, 16, DIRECT), BF16),
+        vm((LON, 128, 128), BF16),
+        vm((LON, 128, 128), F32),
+        vm((LAT - 1, LON, 16, 128), BF16),
+        vm((LON, 16, 128), F32),
+        vm((LON, 16, 128), BF16),
+        vm((LON - 1, 16, 128), BF16),
         vm((4, ROWS, WID), F32),
         vm((3, ROWS, WID), BF16),
         vm((3, ROWS, WID), BF16),
@@ -520,16 +583,18 @@
         dma((7,)), dma((7,)),
         dma((7,)), dma((7,)),
         dma((7,)), dma((7,)),
+        dma((7,)), dma((7,)),
+        dma((7,)), dma((7,)),
         dma((3,)), dma((3,)),
     ]
     in_vmem = pl.BlockSpec(memory_space=pltpu.VMEM)
     anywhere = pl.BlockSpec(memory_space=pl.ANY)
-    d_tok, early, late = pl.pallas_call(
+    d_tok, d_qkv, d_wo = pl.pallas_call(
         kernel,
         out_shape=(
             jax.ShapeDtypeStruct((TH, TW, WID), BF16),
-            jax.ShapeDtypeStruct((16, 2 * WID), F32),
-            jax.ShapeDtypeStruct((16, 2 * WID), F32),
+            jax.ShapeDtypeStruct((3, 16, WID), F32),
+            jax.ShapeDtypeStruct((16, WID), F32),
         ),
         in_specs=[in_vmem, in_vmem, anywhere, anywhere],
         out_specs=(in_vmem, in_vmem, in_vmem),
@@ -544,8 +609,17 @@
         qkv_weight.reshape(3, 4, WID, WID),
         out_weight,
     )
-    d_qkv = jnp.stack([early[:, :WID], late[:, :WID], late[:, WID:]])
-    return d_tok.reshape(tokens.shape), d_qkv, early[:, WID:].T
+    d_tok, d_qkv, d_wo = pl.pallas_call(
+        hand_out,
+        out_shape=(
+            jax.ShapeDtypeStruct((TH, TW, WID), BF16),
+            jax.ShapeDtypeStruct((3, 16, WID), F32),
+            jax.ShapeDtypeStruct((16, WID), F32),
+        ),
+        in_specs=[in_vmem] * 3,
+        out_specs=(in_vmem, in_vmem, in_vmem),
+    )(d_tok, d_qkv, d_wo)
+    return d_tok.reshape(tokens.shape), d_qkv, d_wo.T
 
 
 def solution(mesh):

time: 79.9 us -> 74.1 us (0.927)
  local copies, waits for them, and re-layouts: 3.75 us -> 0 us
  Pallas kernels: 74.6 us -> 73.4 us
    pallas_call x1, Pallas kernels: 74.6 us -> 71.6 us  [local(): pl.pallas_call(kernel, out_shape=(jax.ShapeDtypeStruct((TH, TW, WID), BF1...]
    pallas_call x0 -> x1, Pallas kernels: none -> 1.71 us  [local(): pl.pallas_call(hand_out, out_shape=(jax.ShapeDtypeStruct((TH, TW, WID), B...]
    unnamed x1 -> x0, local copies, waits for them, and re-layouts: 1.67 us -> none
    transpose x1 -> x0, local copies, waits for them, and re-layouts: 1.34 us -> none  [local(): return (d_tok.reshape(tokens.shape), d_qkv, early[:, WID:].T)]
where the time goes in v3:
time: 74.1 us; the launch traced here: 74 us
  Pallas kernels  73.4 us (99%)
    pallas_call x1, Pallas kernels, local(): pl.pallas_call(kernel, out_shape=(jax.ShapeDtypeStruct((TH, TW, WID), BF1...  71.6 us
    pallas_call x1, Pallas kernels, local(): pl.pallas_call(hand_out, out_shape=(jax.ShapeDtypeStruct((TH, TW, WID), B...  1.71 us

profile of v3, /device:TPU:2, one launch (start us, length us, event | category | flops | bytes accessed | tf_op | source)
XLA Modules:
  0.0 74.0 jit_solution(997706177560451720)
XLA Ops:
  0.6 71.6 %shard_map.67 = (bf16[8,64,256]{2,1,0:T(8,128)(2,1)}, f32[3,16,256]{2,1,0:T(8,128)}, f32[16,256]{1,0:T(8,128)}) custom-call(bf16[8,64,256]{2,1,0:T(8,128)(2,1)} %bitcast.6, bf16[8,64,256]{2,1,0:T(8,128)(2,1)} %bitcast.7, bf16[3,4,256,256]{3,2,1,0:T(8,128)(2,1)} %bitcast.5, bf16[256,1024]{1,0:T(8,128)(2,1)} %wo_any.1), custom_call_target="tpu_custom_call" | custom-call | flops 8000000000 | bytes 4000000 | tf_op jit(solution)/shard_map/pallas_call | solution.py:592
  72.3 1.7 %shard_map.68 = (bf16[8,64,256]{2,1,0:T(8,128)(2,1)}, f32[3,16,256]{2,1,0:T(8,128)}, f32[16,256]{1,0:T(8,128)}) custom-call(bf16[8,64,256]{2,1,0:T(8,128)(2,1)} %get-tuple-element.9.tok_in, f32[3,16,256]{2,1,0:T(8,128)} %get-tuple-element.10.dqkv_in, f32[16,256]{1,0:T(8,128)} %get-tuple-element.11.dwo_in), custom_call_target="tpu_custom_call" | custom-call | tf_op jit(solution)/shard_map/pallas_call | solution.py:612

commit v4 on v3

--- a/solution.py
+++ b/solution.py
@@ -39,17 +39,17 @@
 
 
 def kernel(
-    x_ref, g_ref, w_any, wo_any,
+    x_any, g_any, w_any, wo_any,
     tok_ref, dqkv_ref, dwo_ref,
-    w_v, wo_v, xf, gf, kvb, edge, ns_r, ew_r, co_r, kvx, gx,
+    x_ref, g_ref, w_v, wo_v, xf, gf, kvb, edge, ns_r, ew_r, co_r, kvx, gx,
     q_s, do_s, o_s, dq_s, dkv, bias, xt, gt,
     gns_s, gew_s, gns_r, gew_r,
     e_s, e_r, l_s, l_r, own_e, own_l, pe_b, pl_b, e2_r, l2_r,
-    m_s, m_f, m_r, own_m, pm_b, m2_r,
+    m_s, m_f, m_r, own_m, pm_b, m2_r, own_3, e3_s, e3_r,
     tacc, t_s, t_r,
     w_sem, x_ss, x_rs, g_ss, g_rs, n_ss, n_rs, s_ss, s_rs, ew_ss, ew_rs, co_ss, co_rs,
     bn_ss, bn_rs, bs_ss, bs_rs, be_ss, be_rs,
-    e_ss, e_rs, l_ss, l_rs, e2_ss, e2_rs, l2_ss, l2_rs, m_ss, m_rs, m2_ss, m2_rs, t_ss, t_rs,
+    e_ss, e_rs, l_ss, l_rs, e2_ss, e2_rs, l2_ss, l2_rs, m_ss, m_rs, m2_ss, m2_rs, t_ss, t_rs, e3_sem,
 ):
     g = lax.axis_index("grid")
     h = lax.axis_index("heads")
@@ -60,9 +60,13 @@
     opp = 3 - h
     slots = (h, sib, far, opp)
 
+    x_load = pltpu.make_async_copy(x_any, x_ref, w_sem.at[2])
+    g_load = pltpu.make_async_copy(g_any, g_ref, w_sem.at[3])
     w_copy = pltpu.make_async_copy(w_any, w_v, w_sem.at[0])
     wo_copy = pltpu.make_async_copy(wo_any, wo_v, w_sem.at[1])
+    x_load.start()
     w_copy.start()
+    g_load.start()
     wo_copy.start()
 
     def tile(dlat, dlon):
@@ -84,6 +88,7 @@
     for k in range(1, 8):
         greet(tile(k, 0), h)
         greet(tile(0, k), h)
+    x_load.wait()
     pl.semaphore_wait(bar, 16)
 
     def rcopy(src, dst, ss, rs, to_grid, to_head):
@@ -134,6 +139,7 @@
 
         pl.when(jnp.logical_not(can_recv[way]))(blank)
     w_copy.wait()
+    g_load.wait()
 
     def ns_copy(way, c):
         rows = slice(0, SLAB) if way == 0 else slice(QN - SLAB, QN)
@@ -343,28 +349,44 @@
     give(2)
     give(3)
 
-    def e_chunk(chunk):
+    y_at = lax.div(lon, 2)
+    x_at = lax.rem(lon, 2)
+
+    def e_part(chunk):
         dq = dq_s[...].reshape(ROWS, WID)
         oo = o_s[...].reshape(ROWS, WID)
         return jnp.concatenate([mm(xt[chunk], dq), mm(gt[chunk], oo)], axis=1)
 
+    e_plan = ((1, 0, 1), (1, 1, -1), (0, 1, 1), (2, 0, -1), (0, 0, 1), (2, 1, -1))
+
     def e_copy(k):
-        return rcopy(e_s.at[k], e_r.at[k], e_ss.at[k], e_rs.at[k], tile(0, k + 1), h)
+        at, half, to = e_plan[k]
+        return rcopy(e_s.at[at, half], e_r.at[k], e_ss.at[k], e_rs.at[k], tile(0, 2 * to), h)
 
     def l_copy(k):
         return rcopy(l_s.at[k], l_r.at[k], l_ss.at[k], l_rs.at[k], tile(0, k + 1), h)
 
-    def e_step(k, carry):
-        e_s[k] = e_chunk(lax.rem(lon + k + 1, LON)).astype(BF16)
+    def e_fill(at, half):
+        to = lax.rem(y_at + at + 1, LON // 2)
+        e_s[at, half] = e_part(2 * to + half).astype(BF16)
+
+    for k in range(4):
+        at, half, _ = e_plan[k]
+        e_fill(at, half)
         e_copy(k).start()
-        return carry
-
-    lax.fori_loop(0, LON - 1, e_step, 0)
-    own_e[...] = e_chunk(lon)
+    e_fill(0, 0)
+    e_fill(2, 1)
+    for x in range(2):
+        own_e[x] = e_part(2 * y_at + x)
     fold(0)
     give_ew(0)
     fold(4)
     give_ew(1)
+    for k in range(2):
+        e_copy(k).wait_recv()
+        at, half, _ = e_plan[4 + k]
+        e_s[at, half] = (e_s[at, half].astype(F32) + e_r[k].astype(F32)).astype(BF16)
+        e_copy(4 + k).start()
 
     for s in range(4):
         tacc[s] = mm(dq_s[...].reshape(ROWS, WID), w_v[0, s], 1, 1)
@@ -377,28 +399,6 @@
         value = gx[body, PAD + c * BW : PAD + (c + 1) * BW, :].reshape(QN, 2 * WID)
         dkv[c * QN : (c + 1) * QN, :] = value.astype(BF16)
 
-    def m_copy(k):
-        to = lax.rem(lat + k + 1, LAT)
-        rows = pl.ds(pl.multiple_of(to * 16, 16), 16)
-        return rcopy(m_s.at[:, rows], m_r.at[k], m_ss.at[k], m_rs.at[k], tile(k + 1, 0), h)
-
-    def l_step(k, carry):
-        l_s[k] = mm(xt[lax.rem(lon + k + 1, LON)], dkv[:, :DIRECT]).astype(BF16)
-        l_copy(k).start()
-        return carry
-
-    def m_step(k, carry):
-        full = mm(xt[k], dkv[:, DIRECT:])
-        m_s[k] = full.astype(BF16)
-        m_f[k] = full
-        return carry
-
-    lax.fori_loop(0, LON - 1, l_step, 0)
-    lax.fori_loop(0, LON, m_step, 0)
-    for k in range(LAT - 1):
-        m_copy(k).start()
-    own_l[...] = mm(xt[lon], dkv[:, :DIRECT])
-
     def t_full(s):
         return (
             tacc[s]
@@ -411,6 +411,29 @@
     t_far = rcopy(t_s.at[2], t_r.at[2], t_ss.at[2], t_rs.at[2], g, far)
     t_s[0] = t_full(opp).astype(BF16)
     t_opp.start()
+
+    def m_copy(k):
+        to = lax.rem(lat + k + 1, LAT)
+        rows = pl.ds(pl.multiple_of(to * 16, 16), 16)
+        return rcopy(m_s.at[:, rows], m_r.at[k], m_ss.at[k], m_rs.at[k], tile(k + 1, 0), h)
+
+    def l_step(k, carry):
+        l_s[k] = mm(xt[lax.rem(lon + k + 1, LON)], dkv[:, :DIRECT]).astype(BF16)
+        l_copy(k).start()
+        return carry
+
+    def m_step(k, carry):
+        full = mm(xt[k], dkv[:, DIRECT:])
+        m_s[k] = full.astype(BF16)
+        m_f[k] = full
+        return carry
+
+    lax.fori_loop(0, LON - 1, l_step, 0)
+    lax.fori_loop(0, LON, m_step, 0)
+    for k in range(LAT - 1):
+        m_copy(k).start()
+    own_l[...] = mm(xt[lon], dkv[:, :DIRECT])
+
     t_s[1] = t_full(sib).astype(BF16)
     t_sib.start()
     far_part = t_full(far)
@@ -422,7 +445,7 @@
     def e2_copy(k):
         to = lax.rem(lat + k + 1, LAT)
         rows = pl.ds(pl.multiple_of(to * 16, 16), 16)
-        return rcopy(pe_b.at[rows], e2_r.at[k], e2_ss.at[k], e2_rs.at[k], tile(k + 1, 0), h)
+        return rcopy(pe_b.at[:, rows], e2_r.at[k], e2_ss.at[k], e2_rs.at[k], tile(k + 1, 0), h)
 
     def l2_copy(k):
         to = lax.rem(lat + k + 1, LAT)
@@ -448,7 +471,12 @@
         to = lax.rem(lon + k + 1, LON)
         return rcopy(pm_b.at[to], m2_r.at[k], m2_ss.at[k], m2_rs.at[k], tile(0, k + 1), h)
 
-    level(own_e, e_copy, e_r, pe_b, e2_copy)
+    for k in range(2, 6):
+        e_copy(k).wait_recv()
+        own_e[e_plan[k][1]] += e_r[k].astype(F32)
+    pe_b[...] = own_e[...].astype(BF16)
+    for k in range(LAT - 1):
+        e2_copy(k).start()
 
     here = pl.ds(pl.multiple_of(lat * 16, 16), 16)
     total = m_f[:, here, :]
@@ -476,9 +504,14 @@
             total += recv[k].astype(F32)
         return total
 
-    early = finish(own_e, e2_copy, e2_r)
-    dqkv_ref[0] = early[:, :WID]
-    dwo_ref[...] = early[:, WID:]
+    early = own_e[:, here, :]
+    for k in range(LAT - 1):
+        e2_copy(k).wait_recv()
+        early += e2_r[k].astype(F32)
+    own_3[...] = early
+    e3_s[...] = own_3[1 - x_at].astype(BF16)
+    e3_copy = rcopy(e3_s, e3_r, e3_sem.at[0], e3_sem.at[1], tile(0, 1 - 2 * x_at), h)
+    e3_copy.start()
     last = own_m[lon]
     for k in range(LON - 1):
         m2_copy(k).wait_recv()
@@ -487,8 +520,12 @@
     late = finish(own_l, l2_copy, l2_r)
     dqkv_ref[1] = late[:, :WID]
     dqkv_ref[2, :, : WID - 128] = late[:, WID:]
-
-    for copies in x_copies + g_copies + [(t_opp, t_sib, t_far)]:
+    e3_copy.wait_recv()
+    early = own_3[x_at] + e3_r[...].astype(F32)
+    dqkv_ref[0] = early[:, :WID]
+    dwo_ref[...] = early[:, WID:]
+
+    for copies in x_copies + g_copies + [(t_opp, t_sib, t_far, e3_copy)]:
         for copy in copies:
             copy.wait_send()
     for way in range(2):
@@ -505,8 +542,10 @@
 
         pl.when(can_send[way])(sent)
 
+    for k in range(6):
+        e_copy(k).wait_send()
+
     def drain(k, carry):
-        e_copy(k).wait_send()
         l_copy(k).wait_send()
         e2_copy(k).wait_send()
         l2_copy(k).wait_send()
@@ -527,6 +566,8 @@
     vm = pltpu.VMEM
     dma = pltpu.SemaphoreType.DMA
     scratch = [
+        vm((TH, TW, WID), BF16),
+        vm((TH, TW, WID), BF16),
         vm((3, 4, WID, WID), BF16),
         vm((WID, 4 * WID), BF16),
         vm((3, NB, TH, BW, WID), BF16),
@@ -550,15 +591,15 @@
         vm((2, EDGE, 2 * WID), BF16),
         vm((2, PIECES, SLAB, 2 * WID), BF16),
         vm((2, EDGE, 2 * WID), BF16),
-        vm((LON - 1, 128, 2 * WID), BF16),
-        vm((LON - 1, 128, 2 * WID), BF16),
+        vm((LON // 2 - 1, 2, 128, 2 * WID), BF16),
+        vm((6, 128, 2 * WID), BF16),
         vm((LON - 1, 128, DIRECT), BF16),
         vm((LON - 1, 128, DIRECT), BF16),
-        vm((128, 2 * WID), F32),
+        vm((2, 128, 2 * WID), F32),
         vm((128, DIRECT), F32),
-        vm((128, 2 * WID), BF16),
+        vm((2, 128, 2 * WID), BF16),
         vm((128, DIRECT), BF16),
-        vm((LAT - 1, 16, 2 * WID), BF16),
+        vm((LAT - 1, 2, 16, 2 * WID), BF16),
         vm((LAT - 1, 16, DIRECT), BF16),
         vm((LON, 128, 128), BF16),
         vm((LON, 128, 128), F32),
@@ -566,10 +607,13 @@
         vm((LON, 16, 128), F32),
         vm((LON, 16, 128), BF16),
         vm((LON - 1, 16, 128), BF16),
+        vm((2, 16, 2 * WID), F32),
+        vm((16, 2 * WID), BF16),
+        vm((16, 2 * WID), BF16),
         vm((4, ROWS, WID), F32),
         vm((3, ROWS, WID), BF16),
         vm((3, ROWS, WID), BF16),
-        dma((2,)),
+        dma((4,)),
         dma((3 * NB,)), dma((3 * NB,)),
         dma((3 * NB,)), dma((3 * NB,)),
         dma((NB,)), dma((NB,)),
@@ -586,6 +630,7 @@
         dma((7,)), dma((7,)),
         dma((7,)), dma((7,)),
         dma((3,)), dma((3,)),
+        dma((2,)),
     ]
     in_vmem = pl.BlockSpec(memory_space=pltpu.VMEM)
     anywhere = pl.BlockSpec(memory_space=pl.ANY)
@@ -596,7 +641,7 @@
             jax.ShapeDtypeStruct((3, 16, WID), F32),
             jax.ShapeDtypeStruct((16, WID), F32),
         ),
-        in_specs=[in_vmem, in_vmem, anywhere, anywhere],
+        in_specs=[anywhere] * 4,
         out_specs=(in_vmem, in_vmem, in_vmem),
         scratch_shapes=scratch,
         compiler_params=pltpu.CompilerParams(

time: 74.1 us -> 69.2 us (0.934)
  the two profiles are of different devices: /device:TPU:2 before, /device:TPU:4 now
where the time goes in v4:
time: 69.2 us; the launch traced here: 69.1 us
  Pallas kernels  68.4 us (99%)
    pallas_call x1, Pallas kernels, local(): pl.pallas_call(kernel, out_shape=(jax.ShapeDtypeStruct((TH, TW, WID), BF1...  66.7 us
    pallas_call x1, Pallas kernels, local(): pl.pallas_call(hand_out, out_shape=(jax.ShapeDtypeStruct((TH, TW, WID), B...  1.71 us

profile of v4, /device:TPU:4, one launch (start us, length us, event | category | flops | bytes accessed | tf_op | source)
XLA Modules:
  0.0 69.1 jit_solution(8224176694607029438)
XLA Ops:
  0.6 66.7 %shard_map.67 = (bf16[8,64,256]{2,1,0:T(8,128)(2,1)}, f32[3,16,256]{2,1,0:T(8,128)}, f32[16,256]{1,0:T(8,128)}) custom-call(bf16[8,64,256]{2,1,0:T(8,128)(2,1)} %bitcast.6, bf16[8,64,256]{2,1,0:T(8,128)(2,1)} %bitcast.7, bf16[3,4,256,256]{3,2,1,0:T(8,128)(2,1)} %bitcast.5, bf16[256,1024]{1,0:T(8,128)(2,1)} %wo_any.1), custom_call_target="tpu_custom_call" | custom-call | flops 8000000000 | bytes 4000000 | tf_op jit(solution)/shard_map/pallas_call | solution.py:637
  67.4 1.7 %shard_map.68 = (bf16[8,64,256]{2,1,0:T(8,128)(2,1)}, f32[3,16,256]{2,1,0:T(8,128)}, f32[16,256]{1,0:T(8,128)}) custom-call(bf16[8,64,256]{2,1,0:T(8,128)(2,1)} %get-tuple-element.9.tok_in, f32[3,16,256]{2,1,0:T(8,128)} %get-tuple-element.10.dqkv_in, f32[16,256]{1,0:T(8,128)} %get-tuple-element.11.dwo_in), custom_call_target="tpu_custom_call" | custom-call | tf_op jit(solution)/shard_map/pallas_call | solution.py:657

commit v5 on v4

--- a/solution.py
+++ b/solution.py
@@ -207,16 +207,17 @@
             total += mm(chunk_of(x_ref, xf, k, c), w_v[0, slots[k]])
         q_s[c] = total.astype(BF16) * jnp.asarray(HD**-0.5, BF16)
 
-    for c in ORDER[:2]:
-        query(c)
-    for side in range(2):
+    def forward(side):
         ew_copy(side).wait_recv()
         for way in range(2):
             pl.when(can_send[way])(corner_copy(way, side).start)
-    for c in ORDER[2:]:
+
+    for c in ORDER:
         query(c)
+    forward(0)
     for c in range(NB):
         turn(x_ref, xf, xt, c)
+    forward(1)
     for side in range(2):
         cols = slice(PAD + TW, EXT_C) if side == 0 else slice(0, PAD)
         kvx[body, cols, :] = ew_r[side].astype(F32).reshape(TH, PAD, 2 * WID)
@@ -370,18 +371,22 @@
         to = lax.rem(y_at + at + 1, LON // 2)
         e_s[at, half] = e_part(2 * to + half).astype(BF16)
 
-    for k in range(4):
+    for k in range(2):
         at, half, _ = e_plan[k]
         e_fill(at, half)
+        e_copy(k).start()
+    e_fill(0, 1)
+    e_fill(2, 0)
+    fold(0)
+    give_ew(0)
+    fold(4)
+    give_ew(1)
+    for k in range(2, 4):
         e_copy(k).start()
     e_fill(0, 0)
     e_fill(2, 1)
     for x in range(2):
         own_e[x] = e_part(2 * y_at + x)
-    fold(0)
-    give_ew(0)
-    fold(4)
-    give_ew(1)
     for k in range(2):
         e_copy(k).wait_recv()
         at, half, _ = e_plan[4 + k]
@@ -391,7 +396,7 @@
     for s in range(4):
         tacc[s] = mm(dq_s[...].reshape(ROWS, WID), w_v[0, s], 1, 1)
 
-    for p in (1, 2, 3):
+    for p in (2, 1, 3):
         fold(p)
     for way in range(2):
         fold_ew(way)
@@ -516,10 +521,9 @@
     for k in range(LON - 1):
         m2_copy(k).wait_recv()
         last += m2_r[k].astype(F32)
-    dqkv_ref[2, :, WID - 128 :] = last
-    late = finish(own_l, l2_copy, l2_r)
+    late = jnp.concatenate([finish(own_l, l2_copy, l2_r), last], axis=1)
     dqkv_ref[1] = late[:, :WID]
-    dqkv_ref[2, :, : WID - 128] = late[:, WID:]
+    dqkv_ref[2] = late[:, WID:]
     e3_copy.wait_recv()
     early = own_3[x_at] + e3_r[...].astype(F32)
     dqkv_ref[0] = early[:, :WID]
@@ -601,12 +605,12 @@
         vm((128, DIRECT), BF16),
         vm((LAT - 1, 2, 16, 2 * WID), BF16),
         vm((LAT - 1, 16, DIRECT), BF16),
-        vm((LON, 128, 128), BF16),
-        vm((LON, 128, 128), F32),
-        vm((LAT - 1, LON, 16, 128), BF16),
-        vm((LON, 16, 128), F32),
-        vm((LON, 16, 128), BF16),
-        vm((LON - 1, 16, 128), BF16),
+        vm((LON, 128, 2 * WID - DIRECT), BF16),
+        vm((LON, 128, 2 * WID - DIRECT), F32),
+        vm((LAT - 1, LON, 16, 2 * WID - DIRECT), BF16),
+        vm((LON, 16, 2 * WID - DIRECT), F32),
+        vm((LON, 16, 2 * WID - DIRECT), BF16),
+        vm((LON - 1, 16, 2 * WID - DIRECT), BF16),
         vm((2, 16, 2 * WID), F32),
         vm((16, 2 * WID), BF16),
         vm((16, 2 * WID), BF16),

time: 69.2 us -> 68.1 us (0.984)
  the two profiles are of different devices: /device:TPU:4 before, /device:TPU:2 now
where the time goes in v5:
time: 68.1 us; the launch traced here: 67.6 us
  Pallas kernels  66.9 us (98%)
    pallas_call x1, Pallas kernels, local(): pl.pallas_call(kernel, out_shape=(jax.ShapeDtypeStruct((TH, TW, WID), BF1...  65.2 us
    pallas_call x1, Pallas kernels, local(): pl.pallas_call(hand_out, out_shape=(jax.ShapeDtypeStruct((TH, TW, WID), B...  1.71 us

profile of v5, /device:TPU:2, one launch (start us, length us, event | category | flops | bytes accessed | tf_op | source)
XLA Modules:
  0.0 67.6 jit_solution(13154352329177864664)
XLA Ops:
  0.6 65.2 %shard_map.67 = (bf16[8,64,256]{2,1,0:T(8,128)(2,1)}, f32[3,16,256]{2,1,0:T(8,128)}, f32[16,256]{1,0:T(8,128)}) custom-call(bf16[8,64,256]{2,1,0:T(8,128)(2,1)} %bitcast.6, bf16[8,64,256]{2,1,0:T(8,128)(2,1)} %bitcast.7, bf16[3,4,256,256]{3,2,1,0:T(8,128)(2,1)} %bitcast.5, bf16[256,1024]{1,0:T(8,128)(2,1)} %wo_any.1), custom_call_target="tpu_custom_call" | custom-call | flops 8000000000 | bytes 4000000 | tf_op jit(solution)/shard_map/pallas_call | solution.py:641
  65.8 1.7 %shard_map.68 = (bf16[8,64,256]{2,1,0:T(8,128)(2,1)}, f32[3,16,256]{2,1,0:T(8,128)}, f32[16,256]{1,0:T(8,128)}) custom-call(bf16[8,64,256]{2,1,0:T(8,128)(2,1)} %get-tuple-element.9.tok_in, f32[3,16,256]{2,1,0:T(8,128)} %get-tuple-element.10.dqkv_in, f32[16,256]{1,0:T(8,128)} %get-tuple-element.11.dwo_in), custom_call_target="tpu_custom_call" | custom-call | tf_op jit(solution)/shard_map/pallas_call | solution.py:661

commit v6 on v5

--- a/solution.py
+++ b/solution.py
@@ -433,10 +433,10 @@
         m_f[k] = full
         return carry
 
-    lax.fori_loop(0, LON - 1, l_step, 0)
     lax.fori_loop(0, LON, m_step, 0)
     for k in range(LAT - 1):
         m_copy(k).start()
+    lax.fori_loop(0, LON - 1, l_step, 0)
     own_l[...] = mm(xt[lon], dkv[:, :DIRECT])
 
     t_s[1] = t_full(sib).astype(BF16)

time: 68.1 us -> 67.2 us (0.987)
  Pallas kernels: 66.9 us -> 66.1 us
    pallas_call x1, Pallas kernels: 65.2 us -> 64.4 us  [local(): pl.pallas_call(kernel, out_shape=(jax.ShapeDtypeStruct((TH, TW, WID), BF1...]
where the time goes in v6:
time: 67.2 us; the launch traced here: 66.8 us
  Pallas kernels  66.1 us (98%)
    pallas_call x1, Pallas kernels, local(): pl.pallas_call(kernel, out_shape=(jax.ShapeDtypeStruct((TH, TW, WID), BF1...  64.4 us
    pallas_call x1, Pallas kernels, local(): pl.pallas_call(hand_out, out_shape=(jax.ShapeDtypeStruct((TH, TW, WID), B...  1.71 us

profile of v6, /device:TPU:2, one launch (start us, length us, event | category | flops | bytes accessed | tf_op | source)
XLA Modules:
  0.0 66.8 jit_solution(8289104745835094296)
XLA Ops:
  0.6 64.4 %shard_map.67 = (bf16[8,64,256]{2,1,0:T(8,128)(2,1)}, f32[3,16,256]{2,1,0:T(8,128)}, f32[16,256]{1,0:T(8,128)}) custom-call(bf16[8,64,256]{2,1,0:T(8,128)(2,1)} %bitcast.6, bf16[8,64,256]{2,1,0:T(8,128)(2,1)} %bitcast.7, bf16[3,4,256,256]{3,2,1,0:T(8,128)(2,1)} %bitcast.5, bf16[256,1024]{1,0:T(8,128)(2,1)} %wo_any.1), custom_call_target="tpu_custom_call" | custom-call | flops 8000000000 | bytes 4000000 | tf_op jit(solution)/shard_map/pallas_call | solution.py:641
  65.1 1.7 %shard_map.68 = (bf16[8,64,256]{2,1,0:T(8,128)(2,1)}, f32[3,16,256]{2,1,0:T(8,128)}, f32[16,256]{1,0:T(8,128)}) custom-call(bf16[8,64,256]{2,1,0:T(8,128)(2,1)} %get-tuple-element.9.tok_in, f32[3,16,256]{2,1,0:T(8,128)} %get-tuple-element.10.dqkv_in, f32[16,256]{1,0:T(8,128)} %get-tuple-element.11.dwo_in), custom_call_target="tpu_custom_call" | custom-call | tf_op jit(solution)/shard_map/pallas_call | solution.py:661
